TPU v7x, 512 devices: a whole 4x4x16 slice. The times are simulated.
512 devices in a mesh: lat: 8 (over y, z_hi), lon: 64 (over x, z_lo, core).
Axes of the slice: x: 4, y: 4, z: 16 (z_hi: 2, z_lo: 8; z = z_hi * 8 + z_lo), core: 2. Of those that a mesh axis runs over, the one named last changes fastest.
Arguments:
- activations: bfloat16 [2, 48, 768, 192], P(None, 'lat', 'lon'), may hold values from -400 to 400
- cotangent: bfloat16 [2, 48, 768, 192], P(None, 'lat', 'lon'), may hold values from -12 to 12
- gain: float32 [192], replicated, may hold values from 0.5 to 1.5
- w_qkv: bfloat16 [192, 576], replicated, may hold values from -0.4375 to 0.4375
- w_proj: bfloat16 [192, 192], replicated, may hold values from -0.4375 to 0.4375
- bias_table: float32 [8, 6, 3312], P('lat'), may hold values from -3 to 325
- regions: int32 [2, 48, 768], P(None, 'lat', 'lon'), may hold values from 0 to 3
Outputs:
- grad_input: bfloat16 [2, 48, 768, 192], P(None, 'lat', 'lon')
- grad_qkv: float32 [192, 576], replicated
- grad_proj: float32 [192, 192], replicated
- grad_gain: float32 [192], replicated
- grad_table: float32 [8, 6, 3312], P('lat')
All inputs are finite; a program needn't handle non-finite values.
Results may differ from a plain program's by a relative error of at most 0.0094.
The roundings to bfloat16 on the way count: a program that leaves them out, or rounds other values in their place, can miss the bound.
Values may be sent and summed in bfloat16 or wider, within the bound.
A program may use at most 64 MiB of HBM per device.

v0:
```python
import jax
import jax.numpy as jnp
from jax import lax
from jax.sharding import PartitionSpec as P

LEVELS = 2
WIN_LAT = 6
WIN_LON = 12
SHIFT_LAT = 3
SHIFT_LON = 6
REL = 3312


eps_norm = 1e-05
eps_rms = 1e-06


def passed_along(block, axis, distance):
    devices = range(lax.axis_size(axis))
    route = [((i - distance) % len(devices), i) for i in devices]
    return lax.ppermute(block, axis, route)


def pair_index():
    token_ids = jnp.arange(LEVELS * WIN_LAT * WIN_LON, dtype=jnp.int32)
    level_ids = token_ids // (WIN_LAT * WIN_LON)
    row_ids = token_ids // WIN_LON % WIN_LAT
    col_ids = token_ids % WIN_LON
    first_part = (
        (level_ids[:, None] * LEVELS + level_ids[None, :]) * (WIN_LAT * WIN_LAT)
        + row_ids[:, None] * WIN_LAT
        + row_ids[None, :]
    )
    return (
        first_part * (2 * WIN_LON - 1) + col_ids[None, :] - col_ids[:, None] + WIN_LON - 1
    ).reshape(-1)


def to_windows(field_data):
    level_count, row_count, col_count = (
        field_data.shape[0],
        field_data.shape[1],
        field_data.shape[2],
    )
    tail_dims = field_data.shape[3:]
    field_data = field_data.reshape(
        (level_count, row_count // WIN_LAT, WIN_LAT, col_count // WIN_LON, WIN_LON) + tail_dims
    )
    axis_order = (1, 3, 0, 2, 4) + tuple(range(5, 5 + len(tail_dims)))
    field_data = field_data.transpose(axis_order)
    return field_data.reshape(
        (row_count // WIN_LAT * (col_count // WIN_LON), level_count * WIN_LAT * WIN_LON) + tail_dims
    )


def from_windows(windows, row_count, col_count):
    level_count = windows.shape[1] // (WIN_LAT * WIN_LON)
    tail_dims = windows.shape[2:]
    field_data = windows.reshape(
        (row_count // WIN_LAT, col_count // WIN_LON, level_count, WIN_LAT, WIN_LON) + tail_dims
    )
    axis_order = (2, 0, 3, 1, 4) + tuple(range(5, 5 + len(tail_dims)))
    return field_data.transpose(axis_order).reshape((level_count, row_count, col_count) + tail_dims)


def window_grads(wins_x, wins_g, wins_region, wins_bias, gain, w_qkv, w_proj):
    win_count, token_count, feat_width = wins_x.shape
    head_count = wins_bias.shape[1]
    head_dim = feat_width // head_count
    pair_ids = pair_index()
    inputs = wins_x.astype(jnp.float32)
    row_mean = jnp.mean(inputs, axis=-1, keepdims=True)
    centred = inputs - row_mean
    inv_std = lax.rsqrt(jnp.mean(centred * centred, axis=-1, keepdims=True) + eps_norm)
    standard = centred * inv_std
    normed = (standard * gain).astype(jnp.bfloat16)
    flat_normed = normed.reshape(-1, feat_width)
    projected = lax.optimization_barrier(
        jnp.dot(flat_normed, w_qkv, preferred_element_type=jnp.float32).astype(jnp.bfloat16)
    )
    projected = projected.reshape(win_count, token_count, 3, head_count, head_dim)
    queries = projected[:, :, 0].astype(jnp.float32)
    key_vecs = projected[:, :, 1].astype(jnp.float32)
    val_vecs = projected[:, :, 2].astype(jnp.float32)
    score_scale = head_dim ** (-0.5)
    scores = jnp.einsum("nihd,njhd->nhij", queries, key_vecs) * score_scale
    scores = scores + wins_bias[:, :, pair_ids].reshape(
        win_count, head_count, token_count, token_count
    )
    same_region = wins_region[:, None, :, None] == wins_region[:, None, None, :]
    scores = jnp.where(same_region, scores, -1e30)
    row_max = jnp.max(scores, axis=-1, keepdims=True)
    exp_scores = jnp.exp(scores - row_max)
    attn_probs = exp_scores / jnp.sum(exp_scores, axis=-1, keepdims=True)
    probs_low = lax.optimization_barrier(attn_probs.astype(jnp.bfloat16)).astype(jnp.float32)
    mixed = (
        jnp.einsum("nhij,njhd->nihd", probs_low, val_vecs)
        .astype(jnp.bfloat16)
        .reshape(-1, feat_width)
    )
    grad_out = wins_g.reshape(-1, feat_width)
    grad_proj = jnp.dot(mixed.T, grad_out, preferred_element_type=jnp.float32)
    grad_mixed = lax.optimization_barrier(
        jnp.dot(grad_out, w_proj.T, preferred_element_type=jnp.float32).astype(jnp.bfloat16)
    )
    grad_mixed = grad_mixed.astype(jnp.float32).reshape(
        win_count, token_count, head_count, head_dim
    )
    grad_probs = jnp.einsum("nihd,njhd->nhij", grad_mixed, val_vecs)
    grad_values = jnp.einsum("nhij,nihd->njhd", probs_low, grad_mixed).astype(jnp.bfloat16)
    grad_scores = attn_probs * (
        grad_probs - jnp.sum(attn_probs * grad_probs, axis=-1, keepdims=True)
    )
    grad_queries = (jnp.einsum("nhij,njhd->nihd", grad_scores, key_vecs) * score_scale).astype(
        jnp.bfloat16
    )
    grad_keys = (jnp.einsum("nhij,nihd->njhd", grad_scores, queries) * score_scale).astype(
        jnp.bfloat16
    )
    grad_proj_in = jnp.stack([grad_queries, grad_keys, grad_values], axis=2).reshape(
        -1, 3 * feat_width
    )
    grad_qkv = jnp.dot(flat_normed.T, grad_proj_in, preferred_element_type=jnp.float32)
    grad_normed = jnp.dot(grad_proj_in, w_qkv.T, preferred_element_type=jnp.float32).reshape(
        win_count, token_count, feat_width
    )
    grad_gain = jnp.sum(grad_normed * standard, axis=(0, 1))
    grad_std = grad_normed * gain
    grad_x = inv_std * (
        grad_std
        - jnp.mean(grad_std, axis=-1, keepdims=True)
        - standard * jnp.mean(grad_std * standard, axis=-1, keepdims=True)
    )
    return (
        grad_x.astype(jnp.bfloat16),
        grad_qkv,
        grad_proj,
        grad_gain,
        grad_scores.reshape(win_count, head_count, -1),
    )


def rescale(grad_value, squares, entries):
    return grad_value / jnp.sqrt(squares / entries + eps_rms)


def on_device(activations, cotangent, gain, w_qkv, w_proj, bias_table, regions):
    lat_rows = activations.shape[1]
    lon_cols = activations.shape[2]
    band_count = bias_table.shape[0]
    lon_windows = lon_cols // WIN_LON
    border_cols = passed_along(
        (activations[:, :, :SHIFT_LON], cotangent[:, :, :SHIFT_LON]), "lon", -1
    )
    wide_x = jnp.concatenate([activations, border_cols[0]], axis=2)
    wide_g = jnp.concatenate([cotangent, border_cols[1]], axis=2)
    border_rows = passed_along((wide_x[:, :SHIFT_LAT], wide_g[:, :SHIFT_LAT]), "lat", -1)
    full_x = jnp.concatenate([wide_x, border_rows[0]], axis=1)
    full_g = jnp.concatenate([wide_g, border_rows[1]], axis=1)
    rolled = jnp.roll(full_x[:, SHIFT_LAT:, SHIFT_LON:], -1, axis=0)
    rolled_grad = jnp.roll(full_g[:, SHIFT_LAT:, SHIFT_LON:], -1, axis=0)
    wins_bias = jnp.repeat(bias_table, lon_windows, axis=0)
    grad_x, grad_qkv, grad_proj, grad_gain, grad_pairs = window_grads(
        to_windows(rolled),
        to_windows(rolled_grad),
        to_windows(regions),
        wins_bias,
        gain,
        w_qkv,
        w_proj,
    )
    band_pairs = jnp.sum(
        grad_pairs.reshape(band_count, lon_windows, grad_pairs.shape[1], grad_pairs.shape[2]),
        axis=1,
    )
    table_local = (
        jnp.zeros((band_count, bias_table.shape[1], REL), jnp.float32)
        .at[:, :, pair_index()]
        .add(band_pairs)
    )
    grad_rolled = jnp.roll(from_windows(grad_x, lat_rows, lon_cols), 1, axis=0)
    padded = jnp.pad(grad_rolled, ((0, 0), (SHIFT_LAT, 0), (SHIFT_LON, 0), (0, 0)))
    from_south = passed_along(padded[:, lat_rows:], "lat", 1)
    lat_done = jnp.concatenate([from_south, padded[:, SHIFT_LAT:lat_rows]], axis=1)
    from_west = passed_along(lat_done[:, :, lon_cols:], "lon", 1)
    gathered = jnp.concatenate([from_west, lat_done[:, :, SHIFT_LON:lon_cols]], axis=2)
    grad_input = (cotangent.astype(jnp.float32) + gathered.astype(jnp.float32)).astype(jnp.bfloat16)
    lat_count = lax.axis_size("lat")
    table_entries = table_local.size * lat_count
    table_total = lax.psum(table_local, "lon")
    grad_qkv, grad_proj, grad_gain = lax.psum((grad_qkv, grad_proj, grad_gain), ("lat", "lon"))
    table_squares = lax.psum(jnp.sum(table_total * table_total), "lat")
    out_qkv = rescale(grad_qkv, jnp.sum(grad_qkv * grad_qkv), grad_qkv.size)
    out_proj = rescale(grad_proj, jnp.sum(grad_proj * grad_proj), grad_proj.size)
    out_gain = rescale(grad_gain, jnp.sum(grad_gain * grad_gain), grad_gain.size)
    out_table = rescale(table_total, table_squares, table_entries)
    return (grad_input, out_qkv, out_proj, out_gain, out_table)


def solution(mesh):
    in_specs = (
        P(None, "lat", "lon", None),
        P(None, "lat", "lon", None),
        P(),
        P(),
        P(),
        P("lat", None, None),
        P(None, "lat", "lon"),
    )
    out_specs = (P(None, "lat", "lon", None), P(), P(), P(), P("lat", None, None))
    return jax.shard_map(
        on_device, mesh=mesh, in_specs=in_specs, out_specs=out_specs, check_vma=False
    )
```

profile of v0, /device:TPU:1, one launch (start us, length us, event | category | flops | bytes accessed | tf_op | source)
XLA Modules:
  0.0 1636.6 jit_solution(803934033979948621)
XLA Ops:
  8.1 8.8 collective-permute-start
  17.7 9.4 collective-permute-start.2
  27.1 0.9 constant_dynamic-update-slice_fusion.1
  29.8 0.9 constant_dynamic-update-slice_fusion.3
  31.3 38.7 %gather_fusion = f32[20736,6]{1,0:T(8,128)} fusion(f32[6,3312]{0,1:T(8,128)S(1)} %bitcast.72, s32[21504]{0:T(1024)S(1)} %pad_clamp_fusion), kind=kCustom, calls=%fused_computation | custom fusion | bytes 1078272 | tf_op jit(solution)/shard_map/gather | solution.py:87
  70.0 11.6 copy.54
  81.7 10.5 collective-permute-start.1
  92.3 6.1 collective-permute-start.3
  99.2 6.7 collective-permute-done.3
  110.5 6.3 collective-permute-start.4
  117.2 1.1 fusion.42
  119.1 102.4 %psum.37 = f32[192]{0:T(256)S(1)} all-reduce(f32[192]{0:T(256)S(1)} %get-tuple-element.20), channel_id=1, replica_groups=mesh['lat'=8,'lon'=64] {'lat','lon'}, use_global_device_ids=true, to_apply=%region_12.13 | all-reduce | flops 192 | bytes 1536 | tf_op jit(solution)/shard_map/psum | solution.py:191
  223.4 6.2 copy.66
  229.6 113.7 %scatter_custom_fusion = f32[6,3312]{0,1:T(8,128)} fusion(s32[20736]{0:T(1024)S(1)} %fusion.24, f32[20736,6]{1,0:T(8,128)} %copy.66, f32[]{:T(128)} %constant.72.clone.1), kind=kCustom, calls=%fused_computation.22 | custom fusion | flops 124416 | bytes 80000 | tf_op jit(solution)/shard_map/scatter-add | solution.py:179
  344.1 4.2 collective-permute-start.5
  348.4 802.2 %all-reduce.5.cloned.1.call-done = f32[1,6,3312]{1,2,0:T(8,128)} async-done(((f32[1,6,3312]{1,2,0:T(8,128)}), f32[1,6,3312]{1,2,0:T(8,128)}) %all-reduce.5.cloned.1.call-update) | async-done | bytes 79504 | tf_op jit(solution)/shard_map/psum | solution.py:190
  1150.6 2.6 multiply_reduce_fusion
  1153.9 37.5 %psum.39 = f32[]{:T(128)} all-reduce(f32[]{:T(128)} %multiply_reduce_fusion), channel_id=1, replica_groups=mesh['lat'=8,'lon'=64] {'lat'}, use_global_device_ids=true, to_apply=%region_17.18 | all-reduce | flops 1 | bytes 8 | tf_op jit(solution)/shard_map/psum | solution.py:192
  1192.1 1.3 broadcast_divide_fusion
  1193.4 2.6 copy.67
  1196.0 426.5 %all-reduce.7.cloned.1.call-done = (f32[192,576]{1,0:T(8,128)}, f32[192,192]{1,0:T(8,128)}) async-done(((f32[192,576]{1,0:T(8,128)}, f32[192,192]{1,0:T(8,128)}), (f32[192,576]{1,0:T(8,128)}, f32[192,192]{1,0:T(8,128)})) %all-reduce.7.cloned.1.call-update) | async-done | bytes 589840 | tf_op jit(solution)/shard_map/psum | solution.py:191
  1622.5 1.8 multiply_reduce_fusion.2
  1625.0 1.8 broadcast_divide_fusion.2
  1626.8 1.6 multiply_reduce_fusion.3
  (87 shorter events, 13.9 us)
Async XLA Ops:
  7.2 99.4 %copy-start = (bf16[192,576]{1,0:T(8,128)(2,1)S(1)}, bf16[192,576]{1,0:T(8,128)(2,1)}, u32[]{:S(2)}) copy-start(bf16[192,576]{1,0:T(8,128)(2,1)} %param.10) | copy-start | bytes 663556
  7.2 23.6 %copy-start.5 = (f32[1,6,3312]{2,0,1:T(1,128)S(1)}, f32[1,6,3312]{2,0,1:T(1,128)}, u32[]{:S(2)}) copy-start(f32[1,6,3312]{2,0,1:T(1,128)} %param.12) | copy-start | bytes 238468
  7.2 1143.4 %all-reduce.5.cloned.1.call-start = ((), (), s32[]{:S(2)}) async-start(), calls=%async_computation | async-start | bytes 3391488 | tf_op jit(solution)/shard_map/psum | solution.py:190
  8.1 73.5 %collective-permute-start = (bf16[2,6,6,192]{3,0,2,1:T(2,128)(2,1)S(1)}, bf16[2,6,6,192]{3,0,2,1:T(2,128)(2,1)S(1)}, u32[]{:S(2)}, u32[]{:S(2)}) collective-permute-start(bf16[2,6,6,192]{3,0,2,1:T(2,128)(2,1)S(1)} %slice.67), channel_id=1, source_target_pairs={{1,0},{2,1},{3,2},{4,3},{5,4},{6,5},{7,6},{8,7},{9,8},{10,9},{11,1... | collective-permute-start | bytes 82952 | tf_op jit(solution)/shard_map/ppermute | solution.py:21
  17.7 74.6 %collective-permute-start.2 = (bf16[2,6,6,192]{3,0,2,1:T(2,128)(2,1)S(1)}, bf16[2,6,6,192]{3,0,2,1:T(2,128)(2,1)S(1)}, u32[]{:S(2)}, u32[]{:S(2)}) collective-permute-start(bf16[2,6,6,192]{3,0,2,1:T(2,128)(2,1)S(1)} %slice.73), channel_id=1, source_target_pairs={{1,0},{2,1},{3,2},{4,3},{5,4},{6,5},{7,6},{8,7},{9,8},{10,9},{11,1... | collective-permute-start | bytes 82952 | tf_op jit(solution)/shard_map/ppermute | solution.py:21
  81.6 24.6 %copy-start.4 = (bf16[192,192]{1,0:T(8,128)(2,1)S(1)}, bf16[192,192]{1,0:T(8,128)(2,1)}, u32[]{:S(2)}) copy-start(bf16[192,192]{1,0:T(8,128)(2,1)} %param.11) | copy-start | bytes 221188
  81.6 24.9 %copy-start.6 = (f32[192]{0:T(256)S(1)}, f32[192]{0:T(256)}, u32[]{:S(2)}) copy-start(f32[192]{0:T(256)} %param.9) | copy-start | bytes 2308
  81.7 16.7 %collective-permute-start.1 = (bf16[2,3,18,192]{3,0,2,1:T(2,128)(2,1)S(1)}, bf16[2,3,18,192]{3,0,2,1:T(2,128)(2,1)S(1)}, u32[]{:S(2)}, u32[]{:S(2)}) collective-permute-start(bf16[2,3,18,192]{3,0,2,1:T(2,128)(2,1)S(1)} %slice.90), channel_id=1, source_target_pairs={{64,0},{128,64},{192,128},{256,192},{320,256},{384,320},{448,384},... | collective-permute-start | bytes 124424 | tf_op jit(solution)/shard_map/ppermute | solution.py:21
  92.3 13.6 collective-permute-start.3
  110.5 233.6 %collective-permute-start.4 = (bf16[2,3,18,192]{3,0,2,1:T(2,128)(2,1)S(1)}, bf16[2,3,18,192]{3,0,2,1:T(2,128)(2,1)S(1)}, u32[]{:S(2)}, u32[]{:S(2)}) collective-permute-start(bf16[2,3,18,192]{3,0,2,1:T(2,128)(2,1)S(1)} %get-tuple-element.29), channel_id=1, source_target_pairs={{448,0},{0,64},{64,128},{128,192},{192,256},{256,320},{320,384},{3... | collective-permute-start | bytes 124424 | tf_op jit(solution)/shard_map/ppermute | solution.py:21
  343.3 809.9 %copy-start.3 = (bf16[2,6,12,192]{3,0,2,1:T(2,128)(2,1)S(1)}, bf16[2,6,12,192]{3,0,2,1:T(2,128)(2,1)}, u32[]{:S(2)}) copy-start(bf16[2,6,12,192]{3,0,2,1:T(2,128)(2,1)} %param.8) | copy-start | bytes 165892
  343.3 1279.2 %all-reduce.7.cloned.1.call-start = ((), (), s32[]{:S(2)}) async-start(), calls=%async_computation.1 | async-start | bytes 1376256 | tf_op jit(solution)/shard_map/psum | solution.py:191
  344.1 809.1 %collective-permute-start.5 = (bf16[2,6,6,192]{3,0,2,1:T(2,128)(2,1)S(1)}, bf16[2,6,6,192]{3,0,2,1:T(2,128)(2,1)S(1)}, u32[]{:S(2)}, u32[]{:S(2)}) collective-permute-start(bf16[2,6,6,192]{3,0,2,1:T(2,128)(2,1)S(1)} %pad_maximum_fusion.5), channel_id=1, source_target_pairs={{63,0},{0,1},{1,2},{2,3},{3,4},{4,5},{5,6},{6,7},{7,8},{8,9},{9,10... | collective-permute-start | bytes 82952 | tf_op jit(solution)/shard_map/ppermute | solution.py:21
  1150.6 41.5 %copy-start.1 = (f32[1,6,3312]{1,2,0:T(8,128)S(1)}, f32[1,6,3312]{1,2,0:T(8,128)}, u32[]{:S(2)}) copy-start(f32[1,6,3312]{1,2,0:T(8,128)} %all-reduce.5.cloned.1.call-done) | copy-start | bytes 238468
  1622.5 6.6 copy-start.2
Sparse Core Ops, SparseCore 0:
  343.4 807.0 all-reduce.4
  1157.5 464.9 all-reduce.6
where the time goes:
time: 1640 us
  waiting for transfers between devices  1240 us (76%)
  blocking collectives  140 us (9%)
  other arithmetic  128 us (8%)
  local copies, waits for them, and re-layouts  66.5 us (4%)
  starting transfers between devices  45.4 us (3%)
  between operations  17.3 us (1%)
    psum x1, waiting for transfers between devices, on_device(): table_total = lax.psum(table_local, 'lon')  802 us
    psum x1, waiting for transfers between devices, on_device(): lax.psum((grad_qkv, grad_proj, grad_gain), ('lat', 'lon'))  426 us
    scatter-add x1, other arithmetic, on_device(): table_local = jnp.zeros((band_count, bias_table.shape[1], REL), jnp.float...  114 us
    psum x1, blocking collectives, on_device(): lax.psum((grad_qkv, grad_proj, grad_gain), ('lat', 'lon'))  102 us
    ppermute x6, starting transfers between devices, passed_along(): return lax.ppermute(block, axis, route)  45.3 us
    gather x1, local copies, waits for them, and re-layouts, window_grads(): wins_bias[:, :, pair_ids]  38.7 us
    psum x1, blocking collectives, on_device(): table_squares = lax.psum(jnp.sum(table_total * table_total), 'lat')  37.5 us
  transfers between devices with their start and end apart: 8, of which 3 were waited for; matrix products, arithmetic and copies ran while one was open for 11% of the time, Pallas kernels for 0%

commit v1 on v0

v1 whole, which is shorter than its diff:
```python
import functools

import jax
import jax.numpy as jnp
import ml_dtypes
import numpy as np
from jax import lax
from jax.experimental import pallas as pl
from jax.experimental.pallas import tpu as pltpu
from jax.sharding import PartitionSpec as P

F32 = jnp.float32
BF = jnp.bfloat16
MESH = pl.DeviceIdType.MESH

EPS_NORM = 1e-05
EPS_RMS = 1e-06
SCALE = 32.0 ** -0.5

NX, NY, ZHI, ZLO = 4, 4, 2, 8
NZ = ZHI * ZLO
NXY = NX * NY
NLAT = NY * ZHI
NCX = NX * 2


def tables():
    pack = np.zeros((3, 448, 192), np.float32)
    unpack = np.zeros((3, 144, 448), np.float32)
    ret = np.zeros((3, 256, 144), np.float32)
    home = np.zeros((3, 192, 256), np.float32)
    for ah in range(2):
        for bh in range(2):
            q = ah * 2 + bh
            for l in range(2):
                for a3 in range(3):
                    for b6 in range(6):
                        k = l * 18 + a3 * 6 + b6
                        i = a3 + (0 if ah else 3)
                        j = b6 + (0 if bh else 6)
                        src = ((1 - l) * 6 + i) * 16 + j
                        tok = (bh * 6 + b6) * 12 + l * 6 + ah * 3 + a3
                        for c in range(3):
                            pack[c, q * 112 + c * 36 + k, src] = 1
                            unpack[c, tok, q * 112 + c * 36 + k] = 1
                        ret[0, q * 64 + k, tok] = 1
                        home[0, src, q * 64 + k] = 1
                        part = 1 if k < 18 else 2
                        row = q * 64 + 36 + k % 18
                        ret[part, row, tok] = 1
                        home[part, src, row] = 1
    rep = np.zeros((864, 144), np.float32)
    rep[np.arange(864), np.arange(864) // 6] = 1
    heads = np.zeros((864, 192), np.float32)
    heads[np.arange(864)[:, None] % 6 == np.arange(192)[None, :] // 32] = 1
    shift = np.zeros((12, 144, 384), np.float32)
    for bs in range(12):
        for bt in range(12):
            for la in range(12):
                shift[bs, bt * 12 + la, la * 23 + bt - bs + 11] = 1
    rows = np.zeros((192, 256), np.float32)
    for c in range(192):
        rows[c, c // 12 * 16 + c % 12] = 1
    trows = np.zeros((128, 72), np.float32)
    for r in range(72):
        trows[r // 9 * 16 + r % 9, r] = 1
    col = np.zeros((12, 144), np.float32)
    col[np.arange(144) // 12, np.arange(144)] = 1
    lev = np.zeros((2, 6, 144), np.float32)
    for t in range(144):
        lev[t % 12 // 6, t % 6, t] = 1
    colt = col.T.copy()
    levt = lev.transpose(0, 2, 1).copy()
    return [
        m.astype(ml_dtypes.bfloat16)
        for m in (pack, unpack, ret, home, rep, heads, shift, rows, trows, col, lev, colt, levt)
    ]


def mm(a, b):
    return lax.dot_general(a, b, (((1,), (0,)), ((), ())), preferred_element_type=F32)


def mmt(a, b):
    return lax.dot_general(a, b, (((1,), (1,)), ((), ())), preferred_element_type=F32)


def mtm(a, b):
    return lax.dot_general(a, b, (((0,), (0,)), ((), ())), preferred_element_type=F32)


def kernel(
    x_ref, g_ref, gain_ref, wqkv_ref, wproj_ref, table_ref, regions_ref,
    pack_ref, unpack_ref, ret_ref, home_ref, rep_ref, heads_ref, shift_ref, rows_ref, trows_ref,
    col_ref, lev_ref, colt_ref, levt_ref,
    out_x, out_qkv, out_proj, out_gain, out_table,
    xs, gs, zsend, zrecv, osend, orecv, t2, bm,
    main_f, main_s, main_r, xy_f, xy_s, xy_r, z_s, z_r, z_ag, fin,
    tcx_s, tcx_r, tz_s, tz_r, tz_ag, tfin, sq,
    halo_ss, halo_rs, ret_ss, ret_rs, core_ss, core_rs, xy_ss, xy_rs, z_ss, z_rs,
    zag_ss, zag_rs, xyag_ss, xyag_rs, cag_ss, cag_rs,
    tcx_ss, tcx_rs, tz_ss, tz_rs, tzag_ss, tzag_rs, tcag_ss, tcag_rs, sq_ss, sq_rs,
):
    lat = lax.axis_index("lat")
    lon = lax.axis_index("lon")
    nlat, nlon = NLAT, NX * ZLO * 2
    y, z_hi = lat // ZHI, lax.rem(lat, ZHI)
    core = lax.rem(lon, 2)
    chip = lon // 2
    x, z_lo = chip // ZLO, lax.rem(chip, ZLO)
    z = z_hi * ZLO + z_lo
    p = x * NY + y
    cx = x * 2 + core

    def lon_of(x_, z_lo_, core_):
        return (x_ * ZLO + z_lo_) * 2 + core_

    core_peer = (lat, lon_of(x, z_lo, 1 - core))

    def xy_peer(o):
        other = lax.rem(p + o, NXY)
        return other, ((other // NY) * 0 + lax.rem(other, NY) * ZHI + z_hi, lon_of(other // NY, z_lo, core))

    def z_peer(o):
        other = lax.rem(z + o, NZ)
        return other, (y * ZHI + other // ZLO, lon_of(x, lax.rem(other, ZLO), core))

    def cx_peer(o):
        other = lax.rem(cx + o, NCX)
        return other, (lat, lon_of(other // 2, z_lo, lax.rem(other, 2)))

    def zlo_peer(o):
        other = lax.rem(z_lo + o, ZLO)
        return other, (lat, lon_of(x, other, core))

    def lat_peer(o):
        return (lax.rem(lat + o, NLAT), lon)

    before = lambda ah, bh: (lax.rem(lat + nlat - ah, nlat), lax.rem(lon + nlon - bh, nlon))
    after = lambda ah, bh: (lax.rem(lat + ah, nlat), lax.rem(lon + bh, nlon))

    barrier = pltpu.get_barrier_semaphore()

    def greet(device):
        pl.semaphore_signal(barrier, inc=1, device_id=device, device_id_type=MESH)

    greet(core_peer)
    for ah, bh in ((0, 1), (1, 0), (1, 1)):
        greet(before(ah, bh))
        greet(after(ah, bh))

    @pl.loop(1, NXY)
    def _(o):
        greet(xy_peer(o)[1])
        greet(z_peer(o)[1])

    @pl.loop(1, NCX)
    def _(o):
        greet(cx_peer(o)[1])
        greet(lat_peer(o))

    xs[...] = jnp.zeros_like(xs)
    gs[...] = jnp.zeros_like(gs)
    for l in range(2):
        for i in range(6):
            xs[pl.ds((l * 6 + i) * 16, 12), :] = x_ref[l, i]
            gs[pl.ds((l * 6 + i) * 16, 12), :] = g_ref[l, i]
    high = jnp.concatenate([xs[:, 128:192], gs[:, 128:192]], axis=1)
    pieces = mm(pack_ref[0], xs[:, 0:128]) + mm(pack_ref[1], gs[:, 0:128]) + mm(pack_ref[2], high)
    zsend[...] = pieces.astype(BF).reshape(4, 112, 128)
    zrecv[0] = zsend[0]

    pl.semaphore_wait(barrier, 1 + 6 + 2 * (NXY - 1) + 2 * (NCX - 1))

    def remote(src, dst, ss, rs, device):
        return pltpu.make_async_remote_copy(
            src_ref=src, dst_ref=dst, send_sem=ss, recv_sem=rs, device_id=device, device_id_type=MESH
        )

    halo = [
        remote(zsend.at[q], zrecv.at[q], halo_ss.at[q], halo_rs.at[q], before(q // 2, q % 2))
        for q in (1, 2, 3)
    ]
    for c in (halo[2], halo[1], halo[0]):
        c.start()

    t2[...] = jnp.zeros_like(t2)
    for l_s in range(2):
        for a_s in range(6):
            la = l_s * 6 + a_s
            for l_t in range(2):
                off = l_s * 1656 + l_t * 828 + a_s * 138
                t2[pl.ds(la * 6, 6), pl.ds(l_t * 138, 138)] = table_ref[0, :, pl.ds(off, 138)]
    t_all = t2[...]
    t_hi = t_all.astype(BF)
    t_rest = t_all - t_hi.astype(F32)
    t_mid = t_rest.astype(BF)
    t_lo = (t_rest - t_mid.astype(F32)).astype(BF)

    reg_row = jnp.zeros((1, 144), F32)
    reg_col = jnp.zeros((144, 1), F32)
    for l in range(2):
        reg = regions_ref[l].astype(F32).astype(BF)
        reg_row += jnp.sum(mm(reg, col_ref[...]) * lev_ref[l].astype(F32), axis=0, keepdims=True)
        reg_col += jnp.sum(mmt(colt_ref[...], reg) * levt_ref[l].astype(F32), axis=1, keepdims=True)
    same = (reg_row == reg_col).astype(F32).astype(BF)
    for b in range(12):
        sel = shift_ref[b]
        bias = mmt(t_hi, sel) + mmt(t_mid, sel) + mmt(t_lo, sel)
        keep = mm(rep_ref[pl.ds(b * 72, 72), :], same)
        bm[pl.ds(b * 72, 72), :] = jnp.where(keep > 0.5, bias, -1e30)

    for c in halo:
        c.wait_recv()
    zcat = zrecv[...].reshape(448, 128)
    c0 = mm(unpack_ref[0], zcat)
    c1 = mm(unpack_ref[1], zcat)
    c2 = mm(unpack_ref[2], zcat)
    win_x = jnp.concatenate([c0, c2[:, 0:64]], axis=1)
    win_g = jnp.concatenate([c1, c2[:, 64:128]], axis=1).astype(BF)

    gain = gain_ref[...]
    mean = jnp.mean(win_x, axis=-1, keepdims=True)
    centred = win_x - mean
    inv_std = lax.rsqrt(jnp.mean(centred * centred, axis=-1, keepdims=True) + EPS_NORM)
    standard = centred * inv_std
    normed = (standard * gain).astype(BF)
    projected = mm(normed, wqkv_ref[...])
    q = projected[:, 0:192].astype(BF)
    k = projected[:, 192:384].astype(BF)
    v = projected[:, 384:576].astype(BF)
    grad_mixed = mmt(win_g, wproj_ref[...]).astype(BF)

    rep = rep_ref[...]
    heads = heads_ref[...]
    heads_f = heads.astype(F32)
    qm = (mm(rep, q) * heads_f).astype(BF)
    gm = (mm(rep, grad_mixed) * heads_f).astype(BF)
    scores = mmt(qm, k) * SCALE + bm[...]
    top = jnp.max(scores, axis=-1, keepdims=True)
    e = jnp.exp(scores - top)
    probs = e / jnp.sum(e, axis=-1, keepdims=True)
    probs_low = probs.astype(BF)
    grad_probs = mmt(gm, v)
    grad_scores = probs * (grad_probs - jnp.sum(probs * grad_probs, axis=-1, keepdims=True))
    gs_low = grad_scores.astype(BF)
    mixed = mtm(rep, (mm(probs_low, v) * heads_f).astype(BF)).astype(BF)
    gq = mtm(rep, (mm(gs_low, k) * SCALE * heads_f).astype(BF))
    gk = mtm(gs_low, qm) * SCALE
    gv = mtm(probs_low, gm)
    gpi = jnp.concatenate([gq, gk, gv], axis=1).astype(BF)

    normed_pad = mm(normed, rows_ref[...]).astype(BF)
    mixed_pad = mm(mixed, rows_ref[...]).astype(BF)
    g_qkv = mtm(normed_pad, gpi)
    g_proj = mtm(mixed_pad, win_g)
    main_f[0] = g_qkv[:, 0:384]
    main_f[1] = jnp.concatenate([g_qkv[:, 384:576], g_proj], axis=1)
    main_s[...] = main_f[1 - core].astype(BF)
    core_rs_copy = remote(main_s, main_r, core_ss, core_rs, core_peer)
    core_rs_copy.start()

    grad_normed = mmt(gpi, wqkv_ref[...])
    gain_raw = jnp.sum(grad_normed * standard, axis=0, keepdims=True)
    grad_std = grad_normed * gain
    grad_x = inv_std * (
        grad_std
        - jnp.mean(grad_std, axis=-1, keepdims=True)
        - standard * jnp.mean(grad_std * standard, axis=-1, keepdims=True)
    )
    gx_low = grad_x[:, 0:128].astype(BF)
    gx_high = jnp.concatenate([grad_x[:, 128:192], grad_x[:, 128:192]], axis=1).astype(BF)
    lane = lax.broadcasted_iota(jnp.int32, (256, 128), 1)
    back = mm(ret_ref[0], gx_low) + jnp.where(lane < 64, mm(ret_ref[1], gx_high), mm(ret_ref[2], gx_high))
    osend[...] = back.astype(BF).reshape(4, 64, 128)
    orecv[0] = osend[0]
    ret_copies = [
        remote(osend.at[q_], orecv.at[q_], ret_ss.at[q_], ret_rs.at[q_], after(q_ // 2, q_ % 2))
        for q_ in (1, 2, 3)
    ]
    for c in (ret_copies[2], ret_copies[1], ret_copies[0]):
        c.start()

    core_rs_copy.wait_recv()
    half = main_f[core] + main_r[...].astype(F32)
    xy_f[...] = half.reshape(16, 16, 384)
    xy_f[0, 12:13, 0:192] = gain_raw
    xy_s[...] = xy_f[...].astype(BF)

    def xy_copy(o):
        other, device = xy_peer(o)
        return remote(xy_s.at[other], xy_r.at[o - 1], xy_ss.at[o - 1], xy_rs.at[o - 1], device)

    @pl.loop(1, NXY)
    def _(o):
        xy_copy(o).start()

    t_acc = jnp.zeros((72, 384), F32)
    for b in range(12):
        t_acc += mm(gs_low[b * 72:(b + 1) * 72, :], shift_ref[b])
    tcx_s[...] = mm(trows_ref[...], t_acc.astype(BF)).astype(BF).reshape(8, 16, 384)

    def tcx_copy(o):
        other, device = cx_peer(o)
        return remote(tcx_s.at[other], tcx_r.at[o - 1], tcx_ss.at[o - 1], tcx_rs.at[o - 1], device)

    @pl.loop(1, NCX)
    def _(o):
        tcx_copy(o).start()

    @pl.loop(1, NXY)
    def _(o):
        xy_copy(o).wait_recv()

    acc = xy_f[p]
    for o in range(NXY - 1):
        acc += xy_r[o].astype(F32)
    for j in range(NZ):
        z_s[j] = acc[j:j + 1, :]

    def z_copy(o):
        other, device = z_peer(o)
        return remote(z_s.at[other], z_r.at[o - 1], z_ss.at[o - 1], z_rs.at[o - 1], device)

    @pl.loop(1, NZ)
    def _(o):
        z_copy(o).start()

    @pl.loop(1, NCX)
    def _(o):
        tcx_copy(o).wait_recv()

    tacc = tcx_s[cx].astype(F32)
    for o in range(NCX - 1):
        tacc += tcx_r[o].astype(F32)
    for j in range(16):
        tz_s[j] = tacc[j:j + 1, :]

    def tz_copy(o):
        other, device = zlo_peer(o)
        return remote(tz_s.at[pl.ds(other * 2, 2)], tz_r.at[o - 1], tz_ss.at[o - 1], tz_rs.at[o - 1], device)

    @pl.loop(1, ZLO)
    def _(o):
        tz_copy(o).start()

    @pl.loop(1, NZ)
    def _(o):
        z_copy(o).wait_recv()

    row = z_s[z]
    for o in range(NZ - 1):
        row += z_r[o]
    z_ag[z] = row

    def zag_copy(o):
        _, device = z_peer(o)
        return remote(z_ag.at[z], z_ag.at[z], zag_ss.at[o - 1], zag_rs.at[o - 1], device)

    @pl.loop(1, NZ)
    def _(o):
        zag_copy(o).start()

    @pl.loop(1, ZLO)
    def _(o):
        tz_copy(o).wait_recv()

    trow = tz_s[pl.ds(z_lo * 2, 2)]
    for o in range(ZLO - 1):
        trow += tz_r[o]
    tz_ag[pl.ds(z_lo * 2, 2)] = trow

    def tzag_copy(o):
        _, device = zlo_peer(o)
        mine = tz_ag.at[pl.ds(z_lo * 2, 2)]
        return remote(mine, mine, tzag_ss.at[o - 1], tzag_rs.at[o - 1], device)

    @pl.loop(1, ZLO)
    def _(o):
        tzag_copy(o).start()

    @pl.loop(1, NZ)
    def _(o):
        other = lax.rem(z + NZ - o, NZ)
        remote(z_ag.at[other], z_ag.at[other], zag_ss.at[o - 1], zag_rs.at[o - 1], z_peer(o)[1]).wait_recv()

    fin[core, p] = jnp.concatenate([z_ag[j] for j in range(NZ)], axis=0).astype(BF)

    def xyag_copy(o):
        _, device = xy_peer(o)
        return remote(fin.at[core, p], fin.at[core, p], xyag_ss.at[o - 1], xyag_rs.at[o - 1], device)

    @pl.loop(1, NXY)
    def _(o):
        xyag_copy(o).start()

    @pl.loop(1, ZLO)
    def _(o):
        other = lax.rem(z_lo + ZLO - o, ZLO)
        theirs = tz_ag.at[pl.ds(other * 2, 2)]
        remote(theirs, theirs, tzag_ss.at[o - 1], tzag_rs.at[o - 1], zlo_peer(o)[1]).wait_recv()

    tfin[cx] = jnp.concatenate([tz_ag[j] for j in range(16)], axis=0).astype(BF)

    def tcag_copy(o):
        _, device = cx_peer(o)
        return remote(tfin.at[cx], tfin.at[cx], tcag_ss.at[o - 1], tcag_rs.at[o - 1], device)

    @pl.loop(1, NCX)
    def _(o):
        tcag_copy(o).start()

    for c in ret_copies:
        c.wait_recv()
    got = orecv[...].reshape(256, 128)
    h0 = mm(home_ref[0], got)
    h1 = mm(home_ref[1], got)
    h2 = mm(home_ref[2], got)
    grad_in = jnp.concatenate([h0, h1[:, 0:64] + h2[:, 64:128]], axis=1) + gs[...].astype(F32)
    grad_in = grad_in.astype(BF)
    for l in range(2):
        for i in range(6):
            r0 = (l * 6 + i) * 16
            out_x[l, i] = grad_in[r0:r0 + 12, :]

    @pl.loop(1, NXY)
    def _(o):
        other = lax.rem(p + NXY - o, NXY)
        slot = fin.at[core, other]
        remote(slot, slot, xyag_ss.at[o - 1], xyag_rs.at[o - 1], xy_peer(o)[1]).wait_recv()

    cag = remote(fin.at[core], fin.at[core], cag_ss, cag_rs, core_peer)
    cag.start()

    @pl.loop(1, NCX)
    def _(o):
        other = lax.rem(cx + NCX - o, NCX)
        slot = tfin.at[other]
        remote(slot, slot, tcag_ss.at[o - 1], tcag_rs.at[o - 1], cx_peer(o)[1]).wait_recv()

    band = mtm(trows_ref[...], tfin[...].reshape(128, 384))
    squares = jnp.sum(jnp.sum(band * band, axis=1, keepdims=True), axis=0, keepdims=True)
    sq[lat] = jnp.broadcast_to(squares, (1, 128))

    def sq_copy(o):
        return remote(sq.at[lat], sq.at[lat], sq_ss.at[o - 1], sq_rs.at[o - 1], lat_peer(o))

    @pl.loop(1, NLAT)
    def _(o):
        sq_copy(o).start()

    other_half = fin.at[1 - core]
    remote(other_half, other_half, cag_ss, cag_rs, core_peer).wait_recv()
    whole = jnp.concatenate([fin[0].reshape(256, 384), fin[1].reshape(256, 384)], axis=1)
    whole = mm(rows_ref[...], whole)
    w_q, w_p = whole[:, 0:576], whole[:, 576:768]
    w_g = fin[0, 0, 12:13, 0:192].astype(F32) + fin[1, 0, 12:13, 0:192].astype(F32)

    def rescaled(value, entries):
        total = jnp.sum(jnp.sum(value * value, axis=1, keepdims=True), axis=0, keepdims=True)
        return value / jnp.sqrt(total / entries + EPS_RMS)

    out_qkv[...] = rescaled(w_q, 192 * 576)
    out_proj[...] = rescaled(w_p, 192 * 192)
    out_gain[...] = rescaled(w_g, 192)

    @pl.loop(1, NLAT)
    def _(o):
        slot = sq.at[lax.rem(lat + NLAT - o, NLAT)]
        remote(slot, slot, sq_ss.at[o - 1], sq_rs.at[o - 1], lat_peer(o)).wait_recv()

    total = sq[0]
    for j in range(1, NLAT):
        total += sq[j]
    band = band / jnp.sqrt(total[:, 0:1] / (NLAT * 6 * 3312) + EPS_RMS)
    for l_s in range(2):
        for a_s in range(6):
            la = l_s * 6 + a_s
            for l_t in range(2):
                off = l_s * 1656 + l_t * 828 + a_s * 138
                out_table[0, :, pl.ds(off, 138)] = band[la * 6:la * 6 + 6, l_t * 138:l_t * 138 + 138]

    for c in halo + ret_copies + [core_rs_copy, cag]:
        c.wait_send()

    @pl.loop(1, NXY)
    def _(o):
        xy_copy(o).wait_send()
        z_copy(o).wait_send()
        zag_copy(o).wait_send()
        xyag_copy(o).wait_send()

    @pl.loop(1, NCX)
    def _(o):
        tcx_copy(o).wait_send()
        tz_copy(o).wait_send()
        tzag_copy(o).wait_send()
        tcag_copy(o).wait_send()
        sq_copy(o).wait_send()


def on_device(activations, cotangent, gain, w_qkv, w_proj, bias_table, regions):
    consts = [jnp.asarray(m) for m in tables()]
    vmem = pl.BlockSpec(memory_space=pltpu.VMEM)
    dma = pltpu.SemaphoreType.DMA
    scratch = [
        pltpu.VMEM((192, 192), BF), pltpu.VMEM((192, 192), BF),
        pltpu.VMEM((4, 112, 128), BF), pltpu.VMEM((4, 112, 128), BF),
        pltpu.VMEM((4, 64, 128), BF), pltpu.VMEM((4, 64, 128), BF),
        pltpu.VMEM((72, 384), F32), pltpu.VMEM((864, 144), F32),
        pltpu.VMEM((2, 256, 384), F32), pltpu.VMEM((256, 384), BF), pltpu.VMEM((256, 384), BF),
        pltpu.VMEM((16, 16, 384), F32), pltpu.VMEM((16, 16, 384), BF), pltpu.VMEM((15, 16, 384), BF),
        pltpu.VMEM((16, 1, 384), F32), pltpu.VMEM((15, 1, 384), F32), pltpu.VMEM((16, 1, 384), F32),
        pltpu.VMEM((2, 16, 16, 384), BF),
        pltpu.VMEM((8, 16, 384), BF), pltpu.VMEM((7, 16, 384), BF),
        pltpu.VMEM((16, 1, 384), F32), pltpu.VMEM((7, 2, 1, 384), F32), pltpu.VMEM((16, 1, 384), F32),
        pltpu.VMEM((8, 16, 384), BF), pltpu.VMEM((8, 1, 128), F32),
        dma((4,)), dma((4,)), dma((4,)), dma((4,)), dma, dma,
        dma((15,)), dma((15,)), dma((15,)), dma((15,)),
        dma((15,)), dma((15,)), dma((15,)), dma((15,)), dma, dma,
        dma((7,)), dma((7,)), dma((7,)), dma((7,)),
        dma((7,)), dma((7,)), dma((7,)), dma((7,)), dma((7,)), dma((7,)),
    ]
    outs = pl.pallas_call(
        kernel,
        out_shape=(
            jax.ShapeDtypeStruct((2, 6, 12, 192), BF),
            jax.ShapeDtypeStruct((192, 576), F32),
            jax.ShapeDtypeStruct((192, 192), F32),
            jax.ShapeDtypeStruct((1, 192), F32),
            jax.ShapeDtypeStruct((1, 6, 3312), F32),
        ),
        in_specs=[vmem] * 20,
        out_specs=(vmem,) * 5,
        scratch_shapes=scratch,
        compiler_params=pltpu.CompilerParams(
            collective_id=0, has_side_effects=True, vmem_limit_bytes=48 * 1024 * 1024
        ),
        name="swin_backward",
    )(activations, cotangent, gain.reshape(1, 192), w_qkv, w_proj, bias_table, regions, *consts)
    return outs[0], outs[1], outs[2], outs[3].reshape(192), outs[4]


def solution(mesh):
    in_specs = (
        P(None, "lat", "lon", None),
        P(None, "lat", "lon", None),
        P(),
        P(),
        P(),
        P("lat", None, None),
        P(None, "lat", "lon"),
    )
    out_specs = (P(None, "lat", "lon", None), P(), P(), P(), P("lat", None, None))
    return jax.shard_map(
        on_device, mesh=mesh, in_specs=in_specs, out_specs=out_specs, check_vma=False
    )
```

time: 1640 us -> 93.4 us (0.06)
  waiting for transfers between devices: 1240 us -> 0 us
  blocking collectives: 140 us -> 0 us
  other arithmetic: 128 us -> 0 us
  Pallas kernels: 0 us -> 70.2 us
  starting transfers between devices: 45.4 us -> 0 us
  local copies, waits for them, and re-layouts: 66.5 us -> 21.5 us
  between operations: 17.3 us -> 0.68 us
    psum x2 -> x0, waiting for transfers between devices: 1230 us -> none  [the longest x1 802 us: on_device(): table_total = lax.psum(table_local, 'lon')]
    psum x2 -> x0, blocking collectives: 140 us -> none  [the longest x1 102 us: on_device(): lax.psum((grad_qkv, grad_proj, grad_gain), ('lat', 'lon'))]
    scatter-add x1 -> x0, other arithmetic: 114 us -> none  [on_device(): table_local = jnp.zeros((band_count, bias_table.shape[1], REL), jnp.float...]
    pallas_call x0 -> x1, Pallas kernels: none -> 70.2 us  [on_device(): pl.pallas_call(kernel, out_shape=(jax.ShapeDtypeStruct((2, 6, 12, 192), B...]
    ppermute x6 -> x0, starting transfers between devices: 45.3 us -> none  [passed_along(): return lax.ppermute(block, axis, route)]
    gather x1 -> x0, local copies, waits for them, and re-layouts: 38.7 us -> none  [window_grads(): wins_bias[:, :, pair_ids]]
  transfers between devices with their start and end apart: 8 -> 0, of which waited for: 3 -> 0; matrix products, arithmetic and copies ran while one was open for 11% -> 0% of each run, Pallas kernels for 0% -> 0%
where the time goes in v1:
time: 93.4 us; the launch traced here: 92.3 us
  Pallas kernels  70.2 us (75%)
  local copies, waits for them, and re-layouts  21.5 us (23%)
    pallas_call x1, Pallas kernels, on_device(): pl.pallas_call(kernel, out_shape=(jax.ShapeDtypeStruct((2, 6, 12, 192), B...  70.2 us
    unnamed x41, local copies, waits for them, and re-layouts  21.5 us

profile of v1, /device:TPU:1, one launch (start us, length us, event | category | flops | bytes accessed | tf_op | source)
XLA Modules:
  0.0 92.3 jit_solution(8450142178284368585)
XLA Ops:
  0.6 0.7 copy.28.regions_ref
  1.3 0.9 copy.25.x_ref
  2.2 0.9 copy.26.g_ref
  3.1 0.9 copy.27.table_ref
  4.0 1.3 %copy-done = bf16[12,144,384]{2,1,0:T(8,128)(2,1)S(1)} copy-done((bf16[12,144,384]{2,1,0:T(8,128)(2,1)S(1)}, bf16[12,144,384]{2,1,0:T(8,128)(2,1)}, u32[]{:S(2)}) %copy-start) | copy-done | bytes 1327128
  5.4 1.1 %copy-done.1 = bf16[3,448,192]{2,1,0:T(8,128)(2,1)S(1)} copy-done((bf16[3,448,192]{2,1,0:T(8,128)(2,1)S(1)}, bf16[3,448,192]{2,1,0:T(8,128)(2,1)}, u32[]{:S(2)}) %copy-start.1) | copy-done | bytes 516120
  6.5 1.0 %copy-done.2 = bf16[864,192]{1,0:T(8,128)(2,1)S(1)} copy-done((bf16[864,192]{1,0:T(8,128)(2,1)S(1)}, bf16[864,192]{1,0:T(8,128)(2,1)}, u32[]{:S(2)}) %copy-start.2) | copy-done | bytes 331800
  7.5 1.0 %copy-done.3 = bf16[864,144]{1,0:T(8,128)(2,1)S(1)} copy-done((bf16[864,144]{1,0:T(8,128)(2,1)S(1)}, bf16[864,144]{1,0:T(8,128)(2,1)}, u32[]{:S(2)}) %copy-start.3) | copy-done | bytes 248856
  8.5 1.0 %copy-done.4 = bf16[3,144,448]{2,1,0:T(8,128)(2,1)S(1)} copy-done((bf16[3,144,448]{2,1,0:T(8,128)(2,1)S(1)}, bf16[3,144,448]{2,1,0:T(8,128)(2,1)}, u32[]{:S(2)}) %copy-start.4) | copy-done | bytes 387096
  9.5 1.0 %copy-done.5 = bf16[3,256,144]{2,1,0:T(8,128)(2,1)S(1)} copy-done((bf16[3,256,144]{2,1,0:T(8,128)(2,1)S(1)}, bf16[3,256,144]{2,1,0:T(8,128)(2,1)}, u32[]{:S(2)}) %copy-start.5) | copy-done | bytes 221208
  10.5 1.0 %copy-done.6 = bf16[3,192,256]{2,1,0:T(8,128)(2,1)S(1)} copy-done((bf16[3,192,256]{2,1,0:T(8,128)(2,1)S(1)}, bf16[3,192,256]{2,1,0:T(8,128)(2,1)}, u32[]{:S(2)}) %copy-start.6) | copy-done | bytes 294936
  11.5 0.9 %copy-done.7 = bf16[192,576]{1,0:T(8,128)(2,1)S(1)} copy-done((bf16[192,576]{1,0:T(8,128)(2,1)S(1)}, bf16[192,576]{1,0:T(8,128)(2,1)}, u32[]{:S(2)}) %copy-start.7) | copy-done | bytes 221208
  12.4 0.9 copy-done.8
  13.3 0.9 copy-done.9
  14.2 0.9 copy-done.10
  15.1 0.8 copy-done.11
  15.8 0.8 copy-done.12
  16.6 0.7 copy-done.13
  17.3 0.7 copy-done.14
  18.0 0.7 copy-done.15
  18.7 70.2 %swin_backward.1 = (bf16[2,6,12,192]{3,2,1,0:T(8,128)(2,1)S(1)}, f32[192,576]{1,0:T(8,128)S(1)}, f32[192,192]{1,0:T(8,128)S(1)}, f32[1,192]{1,0:T(1,128)S(1)}, f32[1,6,3312]{2,1,0:T(8,128)S(1)}) custom-call(bf16[2,6,12,192]{3,2,1,0:T(8,128)(2,1)S(1)} %copy.25.x_ref, bf16[2,6,12,192]{3,2,1,0:T(8,128)(2,1)S(1)} %copy.26.g_ref, f32[1,192]{1,0:T(1,128)S(1)} %bitcast.2, ...), custom_call_target="tpu_custom_call" | custom-call | tf_op jit(solution)/shard_map/swin_backward/pallas_call | solution.py:524
  88.9 0.7 copy.29
  89.6 0.7 copy.30
  90.3 0.8 copy.34
  (18 shorter events, 1.3 us)
Async XLA Ops:
  4.0 1.3 %copy-start = (bf16[12,144,384]{2,1,0:T(8,128)(2,1)S(1)}, bf16[12,144,384]{2,1,0:T(8,128)(2,1)}, u32[]{:S(2)}) copy-start(bf16[12,144,384]{2,1,0:T(8,128)(2,1)} %constant.32.clone.shift_ref) | copy-start | bytes 3981316
  5.4 1.1 %copy-start.1 = (bf16[3,448,192]{2,1,0:T(8,128)(2,1)S(1)}, bf16[3,448,192]{2,1,0:T(8,128)(2,1)}, u32[]{:S(2)}) copy-start(bf16[3,448,192]{2,1,0:T(8,128)(2,1)} %constant.26.clone.pack_ref) | copy-start | bytes 1548292
  6.5 1.0 %copy-start.2 = (bf16[864,192]{1,0:T(8,128)(2,1)S(1)}, bf16[864,192]{1,0:T(8,128)(2,1)}, u32[]{:S(2)}) copy-start(bf16[864,192]{1,0:T(8,128)(2,1)} %constant.31.clone.heads_ref) | copy-start | bytes 995332
  7.5 1.0 %copy-start.3 = (bf16[864,144]{1,0:T(8,128)(2,1)S(1)}, bf16[864,144]{1,0:T(8,128)(2,1)}, u32[]{:S(2)}) copy-start(bf16[864,144]{1,0:T(8,128)(2,1)} %constant.30.clone.rep_ref) | copy-start | bytes 746500
  8.5 1.0 %copy-start.4 = (bf16[3,144,448]{2,1,0:T(8,128)(2,1)S(1)}, bf16[3,144,448]{2,1,0:T(8,128)(2,1)}, u32[]{:S(2)}) copy-start(bf16[3,144,448]{2,1,0:T(8,128)(2,1)} %constant.27.clone.unpack_ref) | copy-start | bytes 1161220
  9.5 1.0 %copy-start.5 = (bf16[3,256,144]{2,1,0:T(8,128)(2,1)S(1)}, bf16[3,256,144]{2,1,0:T(8,128)(2,1)}, u32[]{:S(2)}) copy-start(bf16[3,256,144]{2,1,0:T(8,128)(2,1)} %constant.28.clone.ret_ref) | copy-start | bytes 663556
  10.5 1.0 %copy-start.6 = (bf16[3,192,256]{2,1,0:T(8,128)(2,1)S(1)}, bf16[3,192,256]{2,1,0:T(8,128)(2,1)}, u32[]{:S(2)}) copy-start(bf16[3,192,256]{2,1,0:T(8,128)(2,1)} %constant.29.clone.home_ref) | copy-start | bytes 884740
  11.5 0.9 %copy-start.7 = (bf16[192,576]{1,0:T(8,128)(2,1)S(1)}, bf16[192,576]{1,0:T(8,128)(2,1)}, u32[]{:S(2)}) copy-start(bf16[192,576]{1,0:T(8,128)(2,1)} %wqkv_ref.1) | copy-start | bytes 663556
  12.4 0.9 copy-start.8
  13.3 0.9 copy-start.9
  14.2 0.9 copy-start.10
  15.1 0.8 copy-start.11
  15.8 0.8 copy-start.12
  16.6 0.7 copy-start.13
  17.3 0.7 copy-start.14
  18.0 0.7 copy-start.15

commit v2 on v1

v2 whole, which is shorter than its diff:
```python
import functools

import jax
import jax.numpy as jnp
import ml_dtypes
import numpy as np
from jax import lax
from jax.experimental import pallas as pl
from jax.experimental.pallas import tpu as pltpu
from jax.sharding import PartitionSpec as P

F32 = jnp.float32
BF = jnp.bfloat16
MESH = pl.DeviceIdType.MESH

EPS_NORM = 1e-05
EPS_RMS = 1e-06
SCALE = 32.0 ** -0.5

NX, NY, ZHI, ZLO = 4, 4, 2, 8
NXY = NX * NY
NLAT = NY * ZHI
NCX = NX * 2


def tables():
    tok = np.arange(144)
    ta, tb, tl = tok // 24, tok // 2 % 12, 1 - tok % 2
    la = tl * 6 + ta
    row = np.arange(864)
    rb, rla, rh = row // 72, row // 6 % 12, row % 6
    rep = (rb[:, None] == tb[None, :]) & (rla[:, None] == la[None, :])
    heads = rh[:, None] == np.arange(192)[None, :] // 32
    shift = np.zeros((12, 144, 384), np.float32)
    for bs in range(12):
        shift[bs, tok, la * 23 + tb - bs + 11] = 1
    rows = np.zeros((192, 256), np.float32)
    chan = np.arange(192)
    rows[chan, chan // 12 * 16 + chan % 12] = 1
    trows = np.zeros((128, 72), np.float32)
    r = np.arange(72)
    trows[r // 9 * 16 + r % 9, r] = 1
    col = tb[None, :] == np.arange(12)[:, None]
    lev = (ta[None, None, :] == np.arange(6)[:, None, None]) & (tl[None, None, :] == np.arange(2)[None, :, None])
    colt = col.T
    levt = lev.transpose(0, 2, 1)
    return [
        np.ascontiguousarray(m).astype(ml_dtypes.bfloat16)
        for m in (rep, heads, shift, rows, trows, col, lev, colt, levt)
    ]


def mm(a, b):
    return lax.dot_general(a, b, (((1,), (0,)), ((), ())), preferred_element_type=F32)


def mmt(a, b):
    return lax.dot_general(a, b, (((1,), (1,)), ((), ())), preferred_element_type=F32)


def mtm(a, b):
    return lax.dot_general(a, b, (((0,), (0,)), ((), ())), preferred_element_type=F32)


def kernel(
    x_hbm, g_hbm, gain_hbm, wqkv_hbm, wproj_hbm, table_hbm, regions_hbm,
    rep_hbm, heads_hbm, shift_hbm, rows_hbm, trows_hbm, col_hbm, lev_hbm, colt_hbm, levt_hbm,
    out_x, out_qkv, out_proj, out_gain, out_table,
    gain_ref, wqkv_ref, wproj_ref, table_ref, regions_ref,
    rep_ref, heads_ref, shift_ref, rows_ref, trows_ref, col_ref, lev_ref, colt_ref, levt_ref,
    own_g, wx, wg, gxw, orecv, xs, gs, gx, t1, t2, bm,
    main_f, main_s, main_r, xy_f, xy_s, xy_r, za, zb, piece, fin,
    tcx_s, tcx_r, ta, tb, tfin, sq,
    load_sem, quarter_sem, halo_ss, halo_rs, ret_ss, ret_rs, core_ss, core_rs, xy_ss, xy_rs, za_ss, za_rs, zb_ss, zb_rs,
    xyag_ss, xyag_rs, cag_ss, cag_rs,
    tcx_ss, tcx_rs, ta_ss, ta_rs, tb_ss, tb_rs, tcag_ss, tcag_rs, sq_ss, sq_rs,
):
    lat = lax.axis_index("lat")
    lon = lax.axis_index("lon")
    nlat, nlon = NLAT, NX * ZLO * 2
    y, z_hi = lat // ZHI, lax.rem(lat, ZHI)
    core = lax.rem(lon, 2)
    chip = lon // 2
    x, z_lo = chip // ZLO, lax.rem(chip, ZLO)
    zq, zr = z_hi * 2 + z_lo // 4, lax.rem(z_lo, 4)
    zhalf = z_lo // 4
    p = x * NY + y
    cx = x * 2 + core

    def lon_of(x_, z_lo_, core_):
        return (x_ * ZLO + z_lo_) * 2 + core_

    core_peer = (lat, lon_of(x, z_lo, 1 - core))

    def xy_peer(o):
        other = lax.rem(p + o, NXY)
        return other, ((other // NY) * 0 + lax.rem(other, NY) * ZHI + z_hi, lon_of(other // NY, z_lo, core))

    def zr_peer(o):
        return (lat, lon_of(x, zhalf * 4 + lax.rem(zr + o, 4), core))

    def zq_peer(o):
        other = lax.rem(zq + o, 4)
        return (y * ZHI + other // 2, lon_of(x, lax.rem(other, 2) * 4 + zr, core))

    def cx_peer(o):
        other = lax.rem(cx + o, NCX)
        return other, (lat, lon_of(other // 2, z_lo, lax.rem(other, 2)))

    far_half = (lat, lon_of(x, lax.rem(z_lo + 4, ZLO), core))
    far_hi = (y * ZHI + 1 - z_hi, lon)

    before = lambda ah, bh: (lax.rem(lat + nlat - ah, nlat), lax.rem(lon + nlon - bh, nlon))
    after = lambda ah, bh: (lax.rem(lat + ah, nlat), lax.rem(lon + bh, nlon))

    barrier = pltpu.get_barrier_semaphore()

    def greet(device):
        pl.semaphore_signal(barrier, inc=1, device_id=device, device_id_type=MESH)

    greet(core_peer)
    for ah, bh in ((0, 1), (1, 0), (1, 1)):
        greet(before(ah, bh))
        greet(after(ah, bh))

    @pl.loop(1, NXY)
    def _(o):
        greet(xy_peer(o)[1])

    for o in range(1, 4):
        greet(zr_peer(o))
        greet(zq_peer(o))
        greet((lat, lon_of(lax.rem(x + o, NX), z_lo, 1 - core)))

    pairs = (
        (regions_hbm, regions_ref), (col_hbm, col_ref), (lev_hbm, lev_ref), (colt_hbm, colt_ref), (levt_hbm, levt_ref),
        (rep_hbm, rep_ref), (table_hbm, table_ref), (shift_hbm, shift_ref), (heads_hbm, heads_ref),
        (wqkv_hbm, wqkv_ref), (wproj_hbm, wproj_ref), (gain_hbm, gain_ref), (rows_hbm, rows_ref),
        (trows_hbm, trows_ref), (g_hbm, own_g),
    )
    loads = [pltpu.make_async_copy(src, dst, load_sem.at[n]) for n, (src, dst) in enumerate(pairs)]
    for c in loads:
        c.start()
    quarter = [
        pltpu.make_async_copy(src.at[pl.ds(3, 3), pl.ds(6, 6)], dst.at[pl.ds(0, 3), pl.ds(0, 6)], quarter_sem.at[n])
        for n, (src, dst) in enumerate(((x_hbm, wx), (g_hbm, wg)))
    ]
    for c in quarter:
        c.start()

    pl.semaphore_wait(barrier, 1 + 6 + (NXY - 1) + 9)

    def remote(src, dst, ss, rs, device):
        return pltpu.make_async_remote_copy(
            src_ref=src, dst_ref=dst, send_sem=ss, recv_sem=rs, device_id=device, device_id_type=MESH
        )

    def here(ah, bh):
        return pl.ds(3 - 3 * ah, 3), pl.ds(6 - 6 * bh, 6)

    def there(ah, bh):
        return pl.ds(3 * ah, 3), pl.ds(6 * bh, 6)

    halo = []
    for ah, bh in ((1, 1), (1, 0), (0, 1)):
        for n, (src, dst) in enumerate(((x_hbm, wx), (g_hbm, wg))):
            at = (ah * 2 + bh) * 2 + n
            halo.append(remote(
                src.at[here(ah, bh)], dst.at[there(ah, bh)], halo_ss.at[at], halo_rs.at[at], before(ah, bh)
            ))
    for c in halo:
        c.start()

    for c in loads:
        c.wait()
    t2[...] = jnp.zeros_like(t2)
    for h in range(6):
        t1[h:h + 1, :] = table_ref[h]
    for l_s in range(2):
        for a_s in range(6):
            la = l_s * 6 + a_s
            for l_t in range(2):
                off = l_s * 1656 + l_t * 828 + a_s * 138
                t2[pl.ds(la * 6, 6), pl.ds(l_t * 138, 138)] = t1[:, pl.ds(off, 138)]
    t_all = t2[...]
    t_hi = t_all.astype(BF)
    t_rest = t_all - t_hi.astype(F32)
    t_mid = t_rest.astype(BF)
    t_lo = (t_rest - t_mid.astype(F32)).astype(BF)

    reg_row = jnp.zeros((1, 144), F32)
    reg_col = jnp.zeros((144, 1), F32)
    for i in range(6):
        reg = regions_ref[i].astype(F32).astype(BF)
        reg_row += jnp.sum(mm(reg, col_ref[...]) * lev_ref[i].astype(F32), axis=0, keepdims=True)
        reg_col += jnp.sum(mmt(colt_ref[...], reg) * levt_ref[i].astype(F32), axis=1, keepdims=True)
    same = (reg_row == reg_col).astype(F32).astype(BF)
    for b in range(12):
        sel = shift_ref[b]
        bias = mmt(t_hi, sel) + mmt(t_mid, sel) + mmt(t_lo, sel)
        keep = mm(rep_ref[pl.ds(b * 72, 72), :], same)
        bm[pl.ds(b * 72, 72), :] = jnp.where(keep > 0.5, bias, -1e30)

    for c in quarter:
        c.wait()
    for c in halo:
        c.wait_recv()
    for n in range(72):
        xs[2 * n:2 * n + 2, :] = wx[n // 12, n % 12]
        gs[2 * n:2 * n + 2, :] = wg[n // 12, n % 12]
    win_x = xs[...].astype(F32)
    win_g = gs[...]

    gain = gain_ref[...]
    mean = jnp.mean(win_x, axis=-1, keepdims=True)
    centred = win_x - mean
    inv_std = lax.rsqrt(jnp.mean(centred * centred, axis=-1, keepdims=True) + EPS_NORM)
    standard = centred * inv_std
    normed = (standard * gain).astype(BF)
    projected = mm(normed, wqkv_ref[...])
    q = projected[:, 0:192].astype(BF)
    k = projected[:, 192:384].astype(BF)
    v = projected[:, 384:576].astype(BF)
    grad_mixed = mmt(win_g, wproj_ref[...]).astype(BF)

    rep = rep_ref[...]
    heads = heads_ref[...]
    heads_f = heads.astype(F32)
    qm = (mm(rep, q) * heads_f).astype(BF)
    gm = (mm(rep, grad_mixed) * heads_f).astype(BF)
    scores = mmt(qm, k) * SCALE + bm[...]
    top = jnp.max(scores, axis=-1, keepdims=True)
    e = jnp.exp(scores - top)
    probs = e / jnp.sum(e, axis=-1, keepdims=True)
    probs_low = probs.astype(BF)
    grad_probs = mmt(gm, v)
    grad_scores = probs * (grad_probs - jnp.sum(probs * grad_probs, axis=-1, keepdims=True))
    gs_low = grad_scores.astype(BF)
    mixed = mtm(rep, (mm(probs_low, v) * heads_f).astype(BF)).astype(BF)
    gq = mtm(rep, (mm(gs_low, k) * SCALE * heads_f).astype(BF))
    gk = mtm(gs_low, qm) * SCALE
    gv = mtm(probs_low, gm)
    gpi = jnp.concatenate([gq, gk, gv], axis=1).astype(BF)

    normed_pad = mm(normed, rows_ref[...]).astype(BF)
    mixed_pad = mm(mixed, rows_ref[...]).astype(BF)
    g_qkv = mtm(normed_pad, gpi)
    g_proj = mtm(mixed_pad, win_g)
    main_f[0] = g_qkv[:, 0:384]
    main_f[1] = jnp.concatenate([g_qkv[:, 384:576], g_proj], axis=1)
    main_s[...] = main_f[1 - core].astype(BF)
    core_rs_copy = remote(main_s, main_r, core_ss, core_rs, core_peer)
    core_rs_copy.start()

    grad_normed = mmt(gpi, wqkv_ref[...])
    gain_raw = jnp.sum(grad_normed * standard, axis=0, keepdims=True)
    grad_std = grad_normed * gain
    grad_x = inv_std * (
        grad_std
        - jnp.mean(grad_std, axis=-1, keepdims=True)
        - standard * jnp.mean(grad_std * standard, axis=-1, keepdims=True)
    )
    gx[...] = grad_x.astype(BF)
    for n in range(72):
        gxw[n // 12, n % 12] = gx[2 * n:2 * n + 2, :]
    ret_copies = [
        remote(gxw.at[there(ah, bh)], orecv.at[here(ah, bh)], ret_ss.at[ah * 2 + bh], ret_rs.at[ah * 2 + bh], after(ah, bh))
        for ah, bh in ((1, 1), (1, 0), (0, 1))
    ]
    for c in ret_copies:
        c.start()
    orecv[here(0, 0)] = gxw[there(0, 0)]

    core_rs_copy.wait_recv()
    half = main_f[core] + main_r[...].astype(F32)
    xy_f[...] = half.reshape(16, 16, 384)
    xy_f[0, 12:13, 0:192] = gain_raw
    xy_s[...] = xy_f[...].astype(BF)

    def xy_copy(o):
        other, device = xy_peer(o)
        return remote(xy_s.at[other], xy_r.at[o - 1], xy_ss.at[o - 1], xy_rs.at[o - 1], device)

    @pl.loop(1, NXY)
    def _(o):
        xy_copy(o).start()

    t_acc = jnp.zeros((72, 384), F32)
    for b in range(12):
        t_acc += mm(gs_low[b * 72:(b + 1) * 72, :], shift_ref[b])
    tcx_s[...] = mm(trows_ref[...], t_acc.astype(BF)).astype(BF).reshape(8, 16, 384)

    def tcx_copy(o):
        other, device = cx_peer(o)
        return remote(tcx_s.at[other], tcx_r.at[o - 1], tcx_ss.at[o - 1], tcx_rs.at[o - 1], device)

    @pl.loop(1, NCX)
    def _(o):
        tcx_copy(o).start()

    for c in halo + [core_rs_copy]:
        c.wait_send()

    @pl.loop(1, NCX)
    def _(o):
        tcx_copy(o).wait_recv()

    tacc = tcx_s[cx].astype(F32)
    for o in range(NCX - 1):
        tacc += tcx_r[o].astype(F32)
    ta[zr] = tacc.astype(BF)

    def spread(buf, at, ss, rs, peer, n):
        out = [remote(buf.at[at], buf.at[at], ss.at[o - 1], rs.at[o - 1], peer(o)) for o in range(1, n)]
        into = []
        for o in range(1, n):
            slot = buf.at[lax.rem(at + n - o, n)]
            into.append(remote(slot, slot, ss.at[o - 1], rs.at[o - 1], peer(o)))
        return out, into

    ta_out, ta_in = spread(ta, zr, ta_ss, ta_rs, zr_peer, 4)
    for c in ta_out:
        c.start()

    @pl.loop(1, NXY)
    def _(o):
        xy_copy(o).wait_recv()

    acc = xy_f[p]
    for o in range(NXY - 1):
        acc += xy_r[o].astype(F32)
    za[zr] = acc.astype(BF)
    za_out, za_in = spread(za, zr, za_ss, za_rs, zr_peer, 4)
    for c in za_out:
        c.start()

    for c in ta_in:
        c.wait_recv()
    tsum = ta[0].astype(F32)
    for j in range(1, 4):
        tsum += ta[j].astype(F32)
    tb[zhalf] = tsum.astype(BF)
    tb_out, tb_in = spread(tb, zhalf, tb_ss, tb_rs, lambda o: far_half, 2)
    tb_out[0].start()

    for c in za_in:
        c.wait_recv()
    acc = za[0].astype(F32)
    for j in range(1, 4):
        acc += za[j].astype(F32)
    zb[zq] = acc.astype(BF)
    zb_out, zb_in = spread(zb, zq, zb_ss, zb_rs, zq_peer, 4)
    for c in zb_out:
        c.start()

    tb_in[0].wait_recv()
    tpiece = tb[0].astype(F32) + tb[1].astype(F32)
    tpiece_low = tpiece.astype(BF)
    tpiece = tpiece_low.astype(F32)
    squares = jnp.sum(jnp.sum(tpiece * tpiece, axis=1, keepdims=True), axis=0, keepdims=True)
    sq[z_hi] = jnp.broadcast_to(squares, (1, 128))
    sq_out, sq_in = spread(sq, z_hi, sq_ss, sq_rs, lambda o: far_hi, 2)
    sq_out[0].start()
    tfin[cx] = tpiece_low

    def tcag_copy(o):
        _, device = cx_peer(o)
        return remote(tfin.at[cx], tfin.at[cx], tcag_ss.at[o - 1], tcag_rs.at[o - 1], device)

    @pl.loop(1, NCX)
    def _(o):
        tcag_copy(o).start()

    for c in ret_copies:
        c.wait()
    out_x[...] = (own_g[...].astype(F32) + orecv[...].astype(F32)).astype(BF)

    @pl.loop(1, NXY)
    def _(o):
        xy_copy(o).wait_send()

    @pl.loop(1, NCX)
    def _(o):
        tcx_copy(o).wait_send()

    for c in ta_out + za_out + tb_out:
        c.wait_send()

    for c in zb_in:
        c.wait_recv()
    acc = zb[0].astype(F32)
    for j in range(1, 4):
        acc += zb[j].astype(F32)
    piece[...] = acc
    sq_in[0].wait_recv()
    both = sq[0] + sq[1]
    both_hi = both.astype(BF).astype(F32)
    both_mid = (both - both_hi).astype(BF).astype(F32)
    both_lo = both - both_hi - both_mid
    lane = lax.broadcasted_iota(jnp.int32, (1, 128), 1)
    piece[13:14, 0:128] = jnp.where(
        lane == 0, both_hi, jnp.where(lane == 1, both_mid, jnp.where(lane == 2, both_lo, 0.0))
    )
    fin[core, p] = piece[...].astype(BF)

    def xyag_copy(o):
        _, device = xy_peer(o)
        return remote(fin.at[core, p], fin.at[core, p], xyag_ss.at[o - 1], xyag_rs.at[o - 1], device)

    @pl.loop(1, NXY)
    def _(o):
        xyag_copy(o).start()

    @pl.loop(1, NCX)
    def _(o):
        other = lax.rem(cx + NCX - o, NCX)
        slot = tfin.at[other]
        remote(slot, slot, tcag_ss.at[o - 1], tcag_rs.at[o - 1], cx_peer(o)[1]).wait_recv()

    band = mtm(trows_ref[...], tfin[...].reshape(128, 384))

    @pl.loop(1, NCX)
    def _(o):
        tcag_copy(o).wait_send()

    for c in zb_out + sq_out:
        c.wait_send()

    @pl.loop(1, NXY)
    def _(o):
        other = lax.rem(p + NXY - o, NXY)
        slot = fin.at[core, other]
        remote(slot, slot, xyag_ss.at[o - 1], xyag_rs.at[o - 1], xy_peer(o)[1]).wait_recv()

    cag = remote(fin.at[core], fin.at[core], cag_ss, cag_rs, core_peer)
    cag.start()

    @pl.loop(1, NXY)
    def _(o):
        xyag_copy(o).wait_send()

    other_half = fin.at[1 - core]
    remote(other_half, other_half, cag_ss, cag_rs, core_peer).wait_recv()
    whole = jnp.concatenate([fin[0].reshape(256, 384), fin[1].reshape(256, 384)], axis=1)
    whole = mm(rows_ref[...], whole)
    w_q, w_p = whole[:, 0:576], whole[:, 576:768]
    w_g = fin[0, 0, 12:13, 0:192].astype(F32) + fin[1, 0, 12:13, 0:192].astype(F32)

    def rescaled(value, entries):
        total = jnp.sum(jnp.sum(value * value, axis=1, keepdims=True), axis=0, keepdims=True)
        return value / jnp.sqrt(total / entries + EPS_RMS)

    out_qkv[...] = rescaled(w_q, 192 * 576)
    out_proj[...] = rescaled(w_p, 192 * 192)
    out_gain[...] = rescaled(w_g, 192)

    shares = jnp.zeros((1, 128), F32)
    for c in range(2):
        for j in range(NXY):
            shares += fin[c, j, 13:14, 0:128].astype(F32)
    total = jnp.sum(shares, axis=1, keepdims=True)
    band = band / jnp.sqrt(total / (NLAT * 6 * 3312) + EPS_RMS)
    for l_s in range(2):
        for a_s in range(6):
            la = l_s * 6 + a_s
            for l_t in range(2):
                off = l_s * 1656 + l_t * 828 + a_s * 138
                t1[:, pl.ds(off, 138)] = band[la * 6:la * 6 + 6, l_t * 138:l_t * 138 + 138]
    for h in range(6):
        out_table[h] = t1[h:h + 1, :]
    cag.wait_send()


def hand_over(*refs):
    sem = refs[-1]
    n = (len(refs) - 1) // 2
    copies = [pltpu.make_async_copy(refs[i], refs[n + i], sem.at[i]) for i in range(n)]
    for c in copies:
        c.start()
    for c in copies:
        c.wait()


def on_device(activations, cotangent, gain, w_qkv, w_proj, bias_table, regions):
    consts = [jnp.asarray(m) for m in tables()]
    vmem = pl.BlockSpec(memory_space=pltpu.VMEM)
    hbm = pl.BlockSpec(memory_space=pltpu.HBM)
    dma = pltpu.SemaphoreType.DMA
    operands = [
        activations.transpose(1, 2, 0, 3), cotangent.transpose(1, 2, 0, 3), gain.reshape(1, 192), w_qkv, w_proj,
        bias_table.transpose(1, 0, 2), regions.transpose(1, 0, 2), *consts,
    ]
    scratch = [pltpu.VMEM(o.shape, o.dtype) for o in operands[2:]] + [
        pltpu.VMEM((6, 12, 2, 192), BF), pltpu.VMEM((6, 12, 2, 192), BF), pltpu.VMEM((6, 12, 2, 192), BF),
        pltpu.VMEM((6, 12, 2, 192), BF), pltpu.VMEM((6, 12, 2, 192), BF),
        pltpu.VMEM((144, 192), BF), pltpu.VMEM((144, 192), BF), pltpu.VMEM((144, 192), BF),
        pltpu.VMEM((6, 3312), F32), pltpu.VMEM((72, 384), F32), pltpu.VMEM((864, 144), F32),
        pltpu.VMEM((2, 256, 384), F32), pltpu.VMEM((256, 384), BF), pltpu.VMEM((256, 384), BF),
        pltpu.VMEM((16, 16, 384), F32), pltpu.VMEM((16, 16, 384), BF), pltpu.VMEM((15, 16, 384), BF),
        pltpu.VMEM((4, 16, 384), BF), pltpu.VMEM((4, 16, 384), BF), pltpu.VMEM((16, 384), F32),
        pltpu.VMEM((2, 16, 16, 384), BF),
        pltpu.VMEM((8, 16, 384), BF), pltpu.VMEM((7, 16, 384), BF),
        pltpu.VMEM((4, 16, 384), BF), pltpu.VMEM((2, 16, 384), BF),
        pltpu.VMEM((8, 16, 384), BF), pltpu.VMEM((2, 1, 128), F32),
        dma((15,)), dma((2,)), dma((8,)), dma((8,)), dma((4,)), dma((4,)), dma, dma,
        dma((15,)), dma((15,)), dma((3,)), dma((3,)), dma((3,)), dma((3,)),
        dma((15,)), dma((15,)), dma, dma,
        dma((7,)), dma((7,)), dma((3,)), dma((3,)), dma((1,)), dma((1,)), dma((7,)), dma((7,)), dma((1,)), dma((1,)),
    ]
    shapes = (
        jax.ShapeDtypeStruct((6, 12, 2, 192), BF),
        jax.ShapeDtypeStruct((192, 576), F32),
        jax.ShapeDtypeStruct((192, 192), F32),
        jax.ShapeDtypeStruct((1, 192), F32),
        jax.ShapeDtypeStruct((6, 1, 3312), F32),
    )
    outs = pl.pallas_call(
        kernel,
        out_shape=shapes,
        in_specs=[hbm] * len(operands),
        out_specs=(vmem,) * 5,
        scratch_shapes=scratch,
        compiler_params=pltpu.CompilerParams(
            collective_id=0, has_side_effects=True, vmem_limit_bytes=40 * 1024 * 1024
        ),
        name="swin_backward",
    )(*[pltpu.with_memory_space_constraint(o, pltpu.HBM) for o in operands])
    outs = pl.pallas_call(
        hand_over,
        out_shape=shapes,
        in_specs=[vmem] * 5,
        out_specs=(hbm,) * 5,
        scratch_shapes=[dma((5,))],
        compiler_params=pltpu.CompilerParams(vmem_limit_bytes=32 * 1024 * 1024),
        name="hand_over",
    )(*outs)
    return outs[0].transpose(2, 0, 1, 3), outs[1], outs[2], outs[3].reshape(192), outs[4].transpose(1, 0, 2)


def solution(mesh):
    in_specs = (
        P(None, "lat", "lon", None),
        P(None, "lat", "lon", None),
        P(),
        P(),
        P(),
        P("lat", None, None),
        P(None, "lat", "lon"),
    )
    out_specs = (P(None, "lat", "lon", None), P(), P(), P(), P("lat", None, None))
    return jax.shard_map(
        on_device, mesh=mesh, in_specs=in_specs, out_specs=out_specs, check_vma=False
    )
```

time: 93.4 us -> 67.7 us (0.72); the launches traced: 92.3 us -> 67.6 us
  local copies, waits for them, and re-layouts: 21.5 us -> 0 us
  Pallas kernels: 70.2 us -> 66.9 us
    unnamed x41 -> x0, local copies, waits for them, and re-layouts: 21.5 us -> none
    pallas_call x1 -> x2, Pallas kernels: 70.2 us -> 66.9 us  [the longest x1 66 us: on_device(): pl.pallas_call(kernel, out_shape=shapes, in_specs=[hbm] * len(operands),...]
where the time goes in v2:
time: 67.7 us; the launch traced here: 67.6 us
  Pallas kernels  66.9 us (99%)
    pallas_call x1, Pallas kernels, on_device(): pl.pallas_call(kernel, out_shape=shapes, in_specs=[hbm] * len(operands),...  66 us

profile of v2, /device:TPU:1, one launch (start us, length us, event | category | flops | bytes accessed | tf_op | source)
XLA Modules:
  0.0 67.6 jit_solution(6391352809002971582)
XLA Ops:
  0.6 66.0 %swin_backward.1 = (bf16[6,12,2,192]{3,2,1,0:T(2,128)(2,1)S(1)}, f32[192,576]{1,0:T(8,128)S(1)}, f32[192,192]{1,0:T(8,128)S(1)}, f32[1,192]{1,0:T(1,128)S(1)}, f32[6,1,3312]{2,1,0:T(1,128)S(1)}) custom-call(bf16[6,12,2,192]{3,2,1,0:T(2,128)(2,1)} %bitcast.9, bf16[6,12,2,192]{3,2,1,0:T(2,128)(2,1)} %bitcast.10, f32[1,192]{1,0:T(1,128)} %bitcast.12, ...), custom_call_target="tpu_custom_call" | custom-call | tf_op jit(solution)/shard_map/swin_backward/pallas_call | solution.py:517
  66.6 0.9 %hand_over.1 = (bf16[6,12,2,192]{3,2,1,0:T(2,128)(2,1)}, f32[192,576]{1,0:T(8,128)}, f32[192,192]{1,0:T(8,128)}, f32[1,192]{1,0:T(1,128)}, f32[6,1,3312]{2,1,0:T(1,128)}) custom-call(bf16[6,12,2,192]{3,2,1,0:T(2,128)(2,1)S(1)} %get-tuple-element.15.refs_0_, f32[192,576]{1,0:T(8,128)S(1)} %get-tuple-element.16.refs_1_, ...), custom_call_target="tpu_custom_call" | custom-call | tf_op jit(solution)/shard_map/hand_over/pallas_call | solution.py:528

commit v3 on v2

--- a/solution.py
+++ b/solution.py
@@ -42,11 +42,9 @@
     trows[r // 9 * 16 + r % 9, r] = 1
     col = tb[None, :] == np.arange(12)[:, None]
     lev = (ta[None, None, :] == np.arange(6)[:, None, None]) & (tl[None, None, :] == np.arange(2)[None, :, None])
-    colt = col.T
-    levt = lev.transpose(0, 2, 1)
     return [
         np.ascontiguousarray(m).astype(ml_dtypes.bfloat16)
-        for m in (rep, heads, shift, rows, trows, col, lev, colt, levt)
+        for m in (rep, heads, shift, rows, trows, col, lev)
     ]
 
 
@@ -64,14 +62,14 @@
 
 def kernel(
     x_hbm, g_hbm, gain_hbm, wqkv_hbm, wproj_hbm, table_hbm, regions_hbm,
-    rep_hbm, heads_hbm, shift_hbm, rows_hbm, trows_hbm, col_hbm, lev_hbm, colt_hbm, levt_hbm,
+    rep_hbm, heads_hbm, shift_hbm, rows_hbm, trows_hbm, col_hbm, lev_hbm,
     out_x, out_qkv, out_proj, out_gain, out_table,
     gain_ref, wqkv_ref, wproj_ref, table_ref, regions_ref,
-    rep_ref, heads_ref, shift_ref, rows_ref, trows_ref, col_ref, lev_ref, colt_ref, levt_ref,
-    own_g, wx, wg, gxw, orecv, xs, gs, gx, t1, t2, bm,
+    rep_ref, heads_ref, shift_ref, rows_ref, trows_ref, col_ref, lev_ref,
+    own_x, own_g, reg_s, reg_r, wx, wg, gxw, orecv, xs, gs, gx, t1, t2, bm,
     main_f, main_s, main_r, xy_f, xy_s, xy_r, za, zb, piece, fin,
     tcx_s, tcx_r, ta, tb, tfin, sq,
-    load_sem, quarter_sem, halo_ss, halo_rs, ret_ss, ret_rs, core_ss, core_rs, xy_ss, xy_rs, za_ss, za_rs, zb_ss, zb_rs,
+    load_sem, reg_ss, reg_rs, halo_ss, halo_rs, ret_ss, ret_rs, core_ss, core_rs, xy_ss, xy_rs, za_ss, za_rs, zb_ss, zb_rs,
     xyag_ss, xyag_rs, cag_ss, cag_rs,
     tcx_ss, tcx_rs, ta_ss, ta_rs, tb_ss, tb_rs, tcag_ss, tcag_rs, sq_ss, sq_rs,
 ):
@@ -108,20 +106,33 @@
         return other, (lat, lon_of(other // 2, z_lo, lax.rem(other, 2)))
 
     far_half = (lat, lon_of(x, lax.rem(z_lo + 4, ZLO), core))
-    far_hi = (y * ZHI + 1 - z_hi, lon)
-
-    before = lambda ah, bh: (lax.rem(lat + nlat - ah, nlat), lax.rem(lon + nlon - bh, nlon))
-    after = lambda ah, bh: (lax.rem(lat + ah, nlat), lax.rem(lon + bh, nlon))
+    mine = z_hi * 2 + core
+
+    def sq_peer(o):
+        other = lax.rem(mine + o, 4)
+        return (y * ZHI + other // 2, lon_of(x, z_lo, lax.rem(other, 2)))
+
+    def midway(lat_, lon_):
+        chip_ = lon_ // 2
+        x_, z_ = chip_ // ZLO, lax.rem(chip_, ZLO)
+        return (lat_, lon_of(x_, lax.rem(z_ + 4, ZLO), lax.rem(lon_, 2)))
+
+    def to_window(ah, bh):
+        return midway(lax.rem(lat + nlat - ah, nlat), lax.rem(lon + nlon - bh, nlon))
+
+    def from_window(ah, bh):
+        return (lax.rem(lat + ah, nlat), lax.rem(midway(lat, lon)[1] + bh, nlon))
 
     barrier = pltpu.get_barrier_semaphore()
 
     def greet(device):
         pl.semaphore_signal(barrier, inc=1, device_id=device, device_id_type=MESH)
 
+    quarters = ((1, 1), (1, 0), (0, 1), (0, 0))
+    for ah, bh in quarters:
+        greet(from_window(ah, bh))
+        greet(to_window(ah, bh))
     greet(core_peer)
-    for ah, bh in ((0, 1), (1, 0), (1, 1)):
-        greet(before(ah, bh))
-        greet(after(ah, bh))
 
     @pl.loop(1, NXY)
     def _(o):
@@ -131,24 +142,27 @@
         greet(zr_peer(o))
         greet(zq_peer(o))
         greet((lat, lon_of(lax.rem(x + o, NX), z_lo, 1 - core)))
+    greet((y * ZHI + 1 - z_hi, lon_of(x, z_lo, 1 - core)))
 
     pairs = (
-        (regions_hbm, regions_ref), (col_hbm, col_ref), (lev_hbm, lev_ref), (colt_hbm, colt_ref), (levt_hbm, levt_ref),
-        (rep_hbm, rep_ref), (table_hbm, table_ref), (shift_hbm, shift_ref), (heads_hbm, heads_ref),
+        (x_hbm, own_x), (g_hbm, own_g), (regions_hbm, regions_ref), (col_hbm, col_ref), (lev_hbm, lev_ref),
+        (table_hbm, table_ref), (shift_hbm, shift_ref), (rep_hbm, rep_ref), (heads_hbm, heads_ref),
         (wqkv_hbm, wqkv_ref), (wproj_hbm, wproj_ref), (gain_hbm, gain_ref), (rows_hbm, rows_ref),
-        (trows_hbm, trows_ref), (g_hbm, own_g),
+        (trows_hbm, trows_ref),
     )
     loads = [pltpu.make_async_copy(src, dst, load_sem.at[n]) for n, (src, dst) in enumerate(pairs)]
     for c in loads:
         c.start()
-    quarter = [
-        pltpu.make_async_copy(src.at[pl.ds(3, 3), pl.ds(6, 6)], dst.at[pl.ds(0, 3), pl.ds(0, 6)], quarter_sem.at[n])
-        for n, (src, dst) in enumerate(((x_hbm, wx), (g_hbm, wg)))
-    ]
-    for c in quarter:
-        c.start()
-
-    pl.semaphore_wait(barrier, 1 + 6 + (NXY - 1) + 9)
+
+    for c in loads[:5]:
+        c.wait()
+    reg_row = jnp.zeros((1, 144), F32)
+    for i in range(6):
+        reg = regions_ref[i].astype(F32).astype(BF)
+        reg_row += jnp.sum(mm(reg, col_ref[...]) * lev_ref[i].astype(F32), axis=0, keepdims=True)
+    reg_s[...] = reg_row
+
+    pl.semaphore_wait(barrier, 8 + 1 + (NXY - 1) + 10)
 
     def remote(src, dst, ss, rs, device):
         return pltpu.make_async_remote_copy(
@@ -161,17 +175,17 @@
     def there(ah, bh):
         return pl.ds(3 * ah, 3), pl.ds(6 * bh, 6)
 
-    halo = []
-    for ah, bh in ((1, 1), (1, 0), (0, 1)):
-        for n, (src, dst) in enumerate(((x_hbm, wx), (g_hbm, wg))):
+    halo = [remote(reg_s, reg_r, reg_ss, reg_rs, midway(lat, lon))]
+    for ah, bh in quarters:
+        for n, (src, dst) in enumerate(((own_x, wx), (own_g, wg))):
             at = (ah * 2 + bh) * 2 + n
             halo.append(remote(
-                src.at[here(ah, bh)], dst.at[there(ah, bh)], halo_ss.at[at], halo_rs.at[at], before(ah, bh)
+                src.at[here(ah, bh)], dst.at[there(ah, bh)], halo_ss.at[at], halo_rs.at[at], to_window(ah, bh)
             ))
     for c in halo:
         c.start()
 
-    for c in loads:
+    for c in loads[5:]:
         c.wait()
     t2[...] = jnp.zeros_like(t2)
     for h in range(6):
@@ -188,22 +202,19 @@
     t_mid = t_rest.astype(BF)
     t_lo = (t_rest - t_mid.astype(F32)).astype(BF)
 
-    reg_row = jnp.zeros((1, 144), F32)
-    reg_col = jnp.zeros((144, 1), F32)
-    for i in range(6):
-        reg = regions_ref[i].astype(F32).astype(BF)
-        reg_row += jnp.sum(mm(reg, col_ref[...]) * lev_ref[i].astype(F32), axis=0, keepdims=True)
-        reg_col += jnp.sum(mmt(colt_ref[...], reg) * levt_ref[i].astype(F32), axis=1, keepdims=True)
-    same = (reg_row == reg_col).astype(F32).astype(BF)
     for b in range(12):
         sel = shift_ref[b]
-        bias = mmt(t_hi, sel) + mmt(t_mid, sel) + mmt(t_lo, sel)
-        keep = mm(rep_ref[pl.ds(b * 72, 72), :], same)
-        bm[pl.ds(b * 72, 72), :] = jnp.where(keep > 0.5, bias, -1e30)
-
-    for c in quarter:
-        c.wait()
-    for c in halo:
+        bm[pl.ds(b * 72, 72), :] = mmt(t_hi, sel) + mmt(t_mid, sel) + mmt(t_lo, sel)
+    rep = rep_ref[...]
+    heads = heads_ref[...]
+    heads_f = heads.astype(F32)
+
+    halo[0].wait_recv()
+    kind = lax.broadcasted_iota(jnp.int32, (8, 144), 0).astype(F32)
+    which = (reg_r[...] == kind).astype(F32).astype(BF)
+    keep = mm(mmt(rep, which).astype(BF), which)
+
+    for c in halo[1:]:
         c.wait_recv()
     for n in range(72):
         xs[2 * n:2 * n + 2, :] = wx[n // 12, n % 12]
@@ -223,12 +234,9 @@
     v = projected[:, 384:576].astype(BF)
     grad_mixed = mmt(win_g, wproj_ref[...]).astype(BF)
 
-    rep = rep_ref[...]
-    heads = heads_ref[...]
-    heads_f = heads.astype(F32)
     qm = (mm(rep, q) * heads_f).astype(BF)
     gm = (mm(rep, grad_mixed) * heads_f).astype(BF)
-    scores = mmt(qm, k) * SCALE + bm[...]
+    scores = jnp.where(keep > 0.5, mmt(qm, k) * SCALE + bm[...], -1e30)
     top = jnp.max(scores, axis=-1, keepdims=True)
     e = jnp.exp(scores - top)
     probs = e / jnp.sum(e, axis=-1, keepdims=True)
@@ -254,6 +262,33 @@
 
     grad_normed = mmt(gpi, wqkv_ref[...])
     gain_raw = jnp.sum(grad_normed * standard, axis=0, keepdims=True)
+    t_acc = jnp.zeros((72, 384), F32)
+    for b in range(12):
+        t_acc += mm(gs_low[b * 72:(b + 1) * 72, :], shift_ref[b])
+    tcx_s[...] = mm(trows_ref[...], t_acc.astype(BF)).astype(BF).reshape(8, 16, 384)
+
+    def tcx_copy(o):
+        other, device = cx_peer(o)
+        return remote(tcx_s.at[other], tcx_r.at[o - 1], tcx_ss.at[o - 1], tcx_rs.at[o - 1], device)
+
+    @pl.loop(1, NCX)
+    def _(o):
+        tcx_copy(o).start()
+
+    core_rs_copy.wait_recv()
+    half = main_f[core] + main_r[...].astype(F32)
+    xy_f[...] = half.reshape(16, 16, 384)
+    xy_f[0, 12:13, 0:192] = gain_raw
+    xy_s[...] = xy_f[...].astype(BF)
+
+    def xy_copy(o):
+        other, device = xy_peer(o)
+        return remote(xy_s.at[other], xy_r.at[o - 1], xy_ss.at[o - 1], xy_rs.at[o - 1], device)
+
+    @pl.loop(1, NXY)
+    def _(o):
+        xy_copy(o).start()
+
     grad_std = grad_normed * gain
     grad_x = inv_std * (
         grad_std
@@ -264,39 +299,11 @@
     for n in range(72):
         gxw[n // 12, n % 12] = gx[2 * n:2 * n + 2, :]
     ret_copies = [
-        remote(gxw.at[there(ah, bh)], orecv.at[here(ah, bh)], ret_ss.at[ah * 2 + bh], ret_rs.at[ah * 2 + bh], after(ah, bh))
-        for ah, bh in ((1, 1), (1, 0), (0, 1))
+        remote(gxw.at[there(ah, bh)], orecv.at[here(ah, bh)], ret_ss.at[ah * 2 + bh], ret_rs.at[ah * 2 + bh], from_window(ah, bh))
+        for ah, bh in quarters
     ]
     for c in ret_copies:
         c.start()
-    orecv[here(0, 0)] = gxw[there(0, 0)]
-
-    core_rs_copy.wait_recv()
-    half = main_f[core] + main_r[...].astype(F32)
-    xy_f[...] = half.reshape(16, 16, 384)
-    xy_f[0, 12:13, 0:192] = gain_raw
-    xy_s[...] = xy_f[...].astype(BF)
-
-    def xy_copy(o):
-        other, device = xy_peer(o)
-        return remote(xy_s.at[other], xy_r.at[o - 1], xy_ss.at[o - 1], xy_rs.at[o - 1], device)
-
-    @pl.loop(1, NXY)
-    def _(o):
-        xy_copy(o).start()
-
-    t_acc = jnp.zeros((72, 384), F32)
-    for b in range(12):
-        t_acc += mm(gs_low[b * 72:(b + 1) * 72, :], shift_ref[b])
-    tcx_s[...] = mm(trows_ref[...], t_acc.astype(BF)).astype(BF).reshape(8, 16, 384)
-
-    def tcx_copy(o):
-        other, device = cx_peer(o)
-        return remote(tcx_s.at[other], tcx_r.at[o - 1], tcx_ss.at[o - 1], tcx_rs.at[o - 1], device)
-
-    @pl.loop(1, NCX)
-    def _(o):
-        tcx_copy(o).start()
 
     for c in halo + [core_rs_copy]:
         c.wait_send()
@@ -358,9 +365,10 @@
     tpiece_low = tpiece.astype(BF)
     tpiece = tpiece_low.astype(F32)
     squares = jnp.sum(jnp.sum(tpiece * tpiece, axis=1, keepdims=True), axis=0, keepdims=True)
-    sq[z_hi] = jnp.broadcast_to(squares, (1, 128))
-    sq_out, sq_in = spread(sq, z_hi, sq_ss, sq_rs, lambda o: far_hi, 2)
-    sq_out[0].start()
+    sq[mine] = jnp.broadcast_to(squares, (1, 128))
+    sq_out, sq_in = spread(sq, mine, sq_ss, sq_rs, sq_peer, 4)
+    for c in sq_out:
+        c.start()
     tfin[cx] = tpiece_low
 
     def tcag_copy(o):
@@ -392,8 +400,9 @@
     for j in range(1, 4):
         acc += zb[j].astype(F32)
     piece[...] = acc
-    sq_in[0].wait_recv()
-    both = sq[0] + sq[1]
+    for c in sq_in:
+        c.wait_recv()
+    both = (sq[0] + sq[1]) + (sq[2] + sq[3])
     both_hi = both.astype(BF).astype(F32)
     both_mid = (both - both_hi).astype(BF).astype(F32)
     both_lo = both - both_hi - both_mid
@@ -439,27 +448,11 @@
     def _(o):
         xyag_copy(o).wait_send()
 
-    other_half = fin.at[1 - core]
-    remote(other_half, other_half, cag_ss, cag_rs, core_peer).wait_recv()
-    whole = jnp.concatenate([fin[0].reshape(256, 384), fin[1].reshape(256, 384)], axis=1)
-    whole = mm(rows_ref[...], whole)
-    w_q, w_p = whole[:, 0:576], whole[:, 576:768]
-    w_g = fin[0, 0, 12:13, 0:192].astype(F32) + fin[1, 0, 12:13, 0:192].astype(F32)
-
-    def rescaled(value, entries):
-        total = jnp.sum(jnp.sum(value * value, axis=1, keepdims=True), axis=0, keepdims=True)
-        return value / jnp.sqrt(total / entries + EPS_RMS)
-
-    out_qkv[...] = rescaled(w_q, 192 * 576)
-    out_proj[...] = rescaled(w_p, 192 * 192)
-    out_gain[...] = rescaled(w_g, 192)
-
     shares = jnp.zeros((1, 128), F32)
-    for c in range(2):
-        for j in range(NXY):
-            shares += fin[c, j, 13:14, 0:128].astype(F32)
+    for j in range(NXY):
+        shares += fin[core, j, 13:14, 0:128].astype(F32)
     total = jnp.sum(shares, axis=1, keepdims=True)
-    band = band / jnp.sqrt(total / (NLAT * 6 * 3312) + EPS_RMS)
+    band = band * (1.0 / jnp.sqrt(total / (NLAT * 6 * 3312) + EPS_RMS))
     for l_s in range(2):
         for a_s in range(6):
             la = l_s * 6 + a_s
@@ -468,6 +461,31 @@
                 t1[:, pl.ds(off, 138)] = band[la * 6:la * 6 + 6, l_t * 138:l_t * 138 + 138]
     for h in range(6):
         out_table[h] = t1[h:h + 1, :]
+
+    def squares_of(value):
+        return jnp.sum(jnp.sum(value * value, axis=1, keepdims=True), axis=0, keepdims=True)
+
+    def part(which_core):
+        value = mm(rows_ref[...], fin[which_core].reshape(256, 384))
+        return value, squares_of(value[:, 0:192]), squares_of(value[:, 192:384]), fin[which_core, 0, 12:13, 0:192].astype(F32)
+
+    own = part(core)
+    other_half = fin.at[1 - core]
+    remote(other_half, other_half, cag_ss, cag_rs, core_peer).wait_recv()
+    theirs = part(1 - core)
+    first = [jnp.where(core == 0, a, b) for a, b in zip(own, theirs)]
+    second = [jnp.where(core == 0, b, a) for a, b in zip(own, theirs)]
+
+    def scale_of(total, entries):
+        return 1.0 / jnp.sqrt(total / entries + EPS_RMS)
+
+    s_qkv = scale_of(first[1] + first[2] + second[1], 192 * 576)
+    s_proj = scale_of(second[2], 192 * 192)
+    out_qkv[:, 0:384] = first[0] * s_qkv
+    out_qkv[:, 384:576] = second[0][:, 0:192] * s_qkv
+    out_proj[...] = second[0][:, 192:384] * s_proj
+    w_g = first[3] + second[3]
+    out_gain[...] = w_g * scale_of(squares_of(w_g), 192)
     cag.wait_send()
 
 
@@ -491,8 +509,8 @@
         bias_table.transpose(1, 0, 2), regions.transpose(1, 0, 2), *consts,
     ]
     scratch = [pltpu.VMEM(o.shape, o.dtype) for o in operands[2:]] + [
-        pltpu.VMEM((6, 12, 2, 192), BF), pltpu.VMEM((6, 12, 2, 192), BF), pltpu.VMEM((6, 12, 2, 192), BF),
-        pltpu.VMEM((6, 12, 2, 192), BF), pltpu.VMEM((6, 12, 2, 192), BF),
+        pltpu.VMEM((6, 12, 2, 192), BF), pltpu.VMEM((6, 12, 2, 192), BF), pltpu.VMEM((1, 144), F32), pltpu.VMEM((1, 144), F32),
+        pltpu.VMEM((6, 12, 2, 192), BF), pltpu.VMEM((6, 12, 2, 192), BF), pltpu.VMEM((6, 12, 2, 192), BF), pltpu.VMEM((6, 12, 2, 192), BF),
         pltpu.VMEM((144, 192), BF), pltpu.VMEM((144, 192), BF), pltpu.VMEM((144, 192), BF),
         pltpu.VMEM((6, 3312), F32), pltpu.VMEM((72, 384), F32), pltpu.VMEM((864, 144), F32),
         pltpu.VMEM((2, 256, 384), F32), pltpu.VMEM((256, 384), BF), pltpu.VMEM((256, 384), BF),
@@ -501,11 +519,11 @@
         pltpu.VMEM((2, 16, 16, 384), BF),
         pltpu.VMEM((8, 16, 384), BF), pltpu.VMEM((7, 16, 384), BF),
         pltpu.VMEM((4, 16, 384), BF), pltpu.VMEM((2, 16, 384), BF),
-        pltpu.VMEM((8, 16, 384), BF), pltpu.VMEM((2, 1, 128), F32),
-        dma((15,)), dma((2,)), dma((8,)), dma((8,)), dma((4,)), dma((4,)), dma, dma,
+        pltpu.VMEM((8, 16, 384), BF), pltpu.VMEM((4, 1, 128), F32),
+        dma((14,)), dma, dma, dma((8,)), dma((8,)), dma((4,)), dma((4,)), dma, dma,
         dma((15,)), dma((15,)), dma((3,)), dma((3,)), dma((3,)), dma((3,)),
         dma((15,)), dma((15,)), dma, dma,
-        dma((7,)), dma((7,)), dma((3,)), dma((3,)), dma((1,)), dma((1,)), dma((7,)), dma((7,)), dma((1,)), dma((1,)),
+        dma((7,)), dma((7,)), dma((3,)), dma((3,)), dma((1,)), dma((1,)), dma((7,)), dma((7,)), dma((3,)), dma((3,)),
     ]
     shapes = (
         jax.ShapeDtypeStruct((6, 12, 2, 192), BF),

time: 67.7 us -> 64.1 us (0.947)
  Pallas kernels: 66.9 us -> 63.4 us
    pallas_call x1, Pallas kernels: 66 us -> 62.4 us  [on_device(): pl.pallas_call(kernel, out_shape=shapes, in_specs=[hbm] * len(operands),...]
where the time goes in v3:
time: 64.1 us; the launch traced here: 64 us
  Pallas kernels  63.4 us (99%)
    pallas_call x1, Pallas kernels, on_device(): pl.pallas_call(kernel, out_shape=shapes, in_specs=[hbm] * len(operands),...  62.4 us

profile of v3, /device:TPU:1, one launch (start us, length us, event | category | flops | bytes accessed | tf_op | source)
XLA Modules:
  0.0 64.0 jit_solution(15136448039890869391)
XLA Ops:
  0.6 62.4 %swin_backward.1 = (bf16[6,12,2,192]{3,2,1,0:T(2,128)(2,1)S(1)}, f32[192,576]{1,0:T(8,128)S(1)}, f32[192,192]{1,0:T(8,128)S(1)}, f32[1,192]{1,0:T(1,128)S(1)}, f32[6,1,3312]{2,1,0:T(1,128)S(1)}) custom-call(bf16[6,12,2,192]{3,2,1,0:T(2,128)(2,1)} %bitcast.9, bf16[6,12,2,192]{3,2,1,0:T(2,128)(2,1)} %bitcast.10, f32[1,192]{1,0:T(1,128)} %bitcast.12, ...), custom_call_target="tpu_custom_call" | custom-call | tf_op jit(solution)/shard_map/swin_backward/pallas_call | solution.py:535
  63.1 0.9 %hand_over.1 = (bf16[6,12,2,192]{3,2,1,0:T(2,128)(2,1)}, f32[192,576]{1,0:T(8,128)}, f32[192,192]{1,0:T(8,128)}, f32[1,192]{1,0:T(1,128)}, f32[6,1,3312]{2,1,0:T(1,128)}) custom-call(bf16[6,12,2,192]{3,2,1,0:T(2,128)(2,1)S(1)} %get-tuple-element.15.refs_0_, f32[192,576]{1,0:T(8,128)S(1)} %get-tuple-element.16.refs_1_, ...), custom_call_target="tpu_custom_call" | custom-call | tf_op jit(solution)/shard_map/hand_over/pallas_call | solution.py:546

commit v4 on v3

--- a/solution.py
+++ b/solution.py
@@ -21,6 +21,8 @@
 NXY = NX * NY
 NLAT = NY * ZHI
 NCX = NX * 2
+OWNERS = [(i, j) for i in range(NX) for j in range(NY) if i != j] + [(0, 0)]
+PIECES = len(OWNERS)
 
 
 def tables():
@@ -34,9 +36,6 @@
     shift = np.zeros((12, 144, 384), np.float32)
     for bs in range(12):
         shift[bs, tok, la * 23 + tb - bs + 11] = 1
-    rows = np.zeros((192, 256), np.float32)
-    chan = np.arange(192)
-    rows[chan, chan // 12 * 16 + chan % 12] = 1
     trows = np.zeros((128, 72), np.float32)
     r = np.arange(72)
     trows[r // 9 * 16 + r % 9, r] = 1
@@ -44,7 +43,7 @@
     lev = (ta[None, None, :] == np.arange(6)[:, None, None]) & (tl[None, None, :] == np.arange(2)[None, :, None])
     return [
         np.ascontiguousarray(m).astype(ml_dtypes.bfloat16)
-        for m in (rep, heads, shift, rows, trows, col, lev)
+        for m in (rep, heads, shift, trows, col, lev)
     ]
 
 
@@ -62,12 +61,12 @@
 
 def kernel(
     x_hbm, g_hbm, gain_hbm, wqkv_hbm, wproj_hbm, table_hbm, regions_hbm,
-    rep_hbm, heads_hbm, shift_hbm, rows_hbm, trows_hbm, col_hbm, lev_hbm,
+    rep_hbm, heads_hbm, shift_hbm, trows_hbm, col_hbm, lev_hbm,
     out_x, out_qkv, out_proj, out_gain, out_table,
     gain_ref, wqkv_ref, wproj_ref, table_ref, regions_ref,
-    rep_ref, heads_ref, shift_ref, rows_ref, trows_ref, col_ref, lev_ref,
-    own_x, own_g, reg_s, reg_r, wx, wg, gxw, orecv, xs, gs, gx, t1, t2, bm,
-    main_f, main_s, main_r, xy_f, xy_s, xy_r, za, zb, piece, fin,
+    rep_ref, heads_ref, shift_ref, trows_ref, col_ref, lev_ref,
+    own_x, own_g, reg_s, reg_r, pack, win, gxw, orecv, xg, gx, t1, t2, bm,
+    main_f, main_s, main_r, xy_f, xy_s, xy_r, za, zb, fin,
     tcx_s, tcx_r, ta, tb, tfin, sq,
     load_sem, reg_ss, reg_rs, halo_ss, halo_rs, ret_ss, ret_rs, core_ss, core_rs, xy_ss, xy_rs, za_ss, za_rs, zb_ss, zb_rs,
     xyag_ss, xyag_rs, cag_ss, cag_rs,
@@ -106,11 +105,15 @@
         return other, (lat, lon_of(other // 2, z_lo, lax.rem(other, 2)))
 
     far_half = (lat, lon_of(x, lax.rem(z_lo + 4, ZLO), core))
-    mine = z_hi * 2 + core
-
-    def sq_peer(o):
-        other = lax.rem(mine + o, 4)
-        return (y * ZHI + other // 2, lon_of(x, z_lo, lax.rem(other, 2)))
+    owner = jnp.logical_or(x != y, x == 0)
+    w = jnp.where(x == y, PIECES - 1, x * (NY - 1) + y - (y > x).astype(jnp.int32))
+
+    def place(n):
+        i, j = OWNERS[n]
+        return i * NY + j, (j * ZHI + z_hi, lon_of(i, z_lo, core))
+
+    def lat_peer(o):
+        return (lax.rem(lat + o, NLAT), lon)
 
     def midway(lat_, lon_):
         chip_ = lon_ // 2
@@ -142,12 +145,12 @@
         greet(zr_peer(o))
         greet(zq_peer(o))
         greet((lat, lon_of(lax.rem(x + o, NX), z_lo, 1 - core)))
-    greet((y * ZHI + 1 - z_hi, lon_of(x, z_lo, 1 - core)))
+        greet((lax.rem(y + o, NY) * ZHI + 1 - z_hi, lon))
 
     pairs = (
         (x_hbm, own_x), (g_hbm, own_g), (regions_hbm, regions_ref), (col_hbm, col_ref), (lev_hbm, lev_ref),
         (table_hbm, table_ref), (shift_hbm, shift_ref), (rep_hbm, rep_ref), (heads_hbm, heads_ref),
-        (wqkv_hbm, wqkv_ref), (wproj_hbm, wproj_ref), (gain_hbm, gain_ref), (rows_hbm, rows_ref),
+        (wqkv_hbm, wqkv_ref), (wproj_hbm, wproj_ref), (gain_hbm, gain_ref),
         (trows_hbm, trows_ref),
     )
     loads = [pltpu.make_async_copy(src, dst, load_sem.at[n]) for n, (src, dst) in enumerate(pairs)]
@@ -162,7 +165,11 @@
         reg_row += jnp.sum(mm(reg, col_ref[...]) * lev_ref[i].astype(F32), axis=0, keepdims=True)
     reg_s[...] = reg_row
 
-    pl.semaphore_wait(barrier, 8 + 1 + (NXY - 1) + 10)
+    pack[:, :, 0] = own_x[:, :, :, 0:128]
+    pack[:, :, 1] = own_g[:, :, :, 0:128]
+    pack[:, :, 2] = jnp.concatenate([own_x[:, :, :, 128:192], own_g[:, :, :, 128:192]], axis=-1)
+
+    pl.semaphore_wait(barrier, 8 + 1 + (NXY - 1) + 12)
 
     def remote(src, dst, ss, rs, device):
         return pltpu.make_async_remote_copy(
@@ -177,11 +184,10 @@
 
     halo = [remote(reg_s, reg_r, reg_ss, reg_rs, midway(lat, lon))]
     for ah, bh in quarters:
-        for n, (src, dst) in enumerate(((own_x, wx), (own_g, wg))):
-            at = (ah * 2 + bh) * 2 + n
-            halo.append(remote(
-                src.at[here(ah, bh)], dst.at[there(ah, bh)], halo_ss.at[at], halo_rs.at[at], to_window(ah, bh)
-            ))
+        at = ah * 2 + bh
+        halo.append(remote(
+            pack.at[here(ah, bh)], win.at[there(ah, bh)], halo_ss.at[at], halo_rs.at[at], to_window(ah, bh)
+        ))
     for c in halo:
         c.start()
 
@@ -217,10 +223,11 @@
     for c in halo[1:]:
         c.wait_recv()
     for n in range(72):
-        xs[2 * n:2 * n + 2, :] = wx[n // 12, n % 12]
-        gs[2 * n:2 * n + 2, :] = wg[n // 12, n % 12]
-    win_x = xs[...].astype(F32)
-    win_g = gs[...]
+        for c in range(3):
+            xg[2 * n:2 * n + 2, c * 128:c * 128 + 128] = win[n // 12, n % 12, c]
+    high = xg[:, 256:384].astype(F32)
+    win_x = jnp.concatenate([xg[:, 0:128].astype(F32), high[:, 0:64]], axis=1)
+    win_g = jnp.concatenate([xg[:, 128:256].astype(F32), high[:, 64:128]], axis=1).astype(BF)
 
     gain = gain_ref[...]
     mean = jnp.mean(win_x, axis=-1, keepdims=True)
@@ -250,12 +257,9 @@
     gv = mtm(probs_low, gm)
     gpi = jnp.concatenate([gq, gk, gv], axis=1).astype(BF)
 
-    normed_pad = mm(normed, rows_ref[...]).astype(BF)
-    mixed_pad = mm(mixed, rows_ref[...]).astype(BF)
-    g_qkv = mtm(normed_pad, gpi)
-    g_proj = mtm(mixed_pad, win_g)
+    g_qkv = mtm(normed, gpi)
     main_f[0] = g_qkv[:, 0:384]
-    main_f[1] = jnp.concatenate([g_qkv[:, 384:576], g_proj], axis=1)
+    main_f[1] = jnp.concatenate([g_qkv[:, 384:576], mtm(mixed, win_g)], axis=1)
     main_s[...] = main_f[1 - core].astype(BF)
     core_rs_copy = remote(main_s, main_r, core_ss, core_rs, core_peer)
     core_rs_copy.start()
@@ -276,18 +280,23 @@
         tcx_copy(o).start()
 
     core_rs_copy.wait_recv()
-    half = main_f[core] + main_r[...].astype(F32)
-    xy_f[...] = half.reshape(16, 16, 384)
-    xy_f[0, 12:13, 0:192] = gain_raw
+    both_cores = main_f[core] + main_r[...].astype(F32)
+    xy_f[0:PIECES - 1] = both_cores.reshape(PIECES - 1, 16, 384)
+    xy_f[PIECES - 1] = jnp.zeros((16, 384), F32)
+    xy_f[PIECES - 1, 0:1, 0:192] = gain_raw
     xy_s[...] = xy_f[...].astype(BF)
-
-    def xy_copy(o):
-        other, device = xy_peer(o)
-        return remote(xy_s.at[other], xy_r.at[o - 1], xy_ss.at[o - 1], xy_rs.at[o - 1], device)
-
-    @pl.loop(1, NXY)
-    def _(o):
-        xy_copy(o).start()
+    xy_r[p] = jnp.zeros((16, 384), BF)
+
+    def xy_copy(n):
+        at, device = place(n)
+        return at, remote(xy_s.at[n], xy_r.at[p], xy_ss.at[n], xy_rs.at[p], device)
+
+    for n in range(PIECES):
+        at, c = xy_copy(n)
+
+        @pl.when(p != at)
+        def _(c=c):
+            c.start()
 
     grad_std = grad_normed * gain
     grad_x = inv_std * (
@@ -302,8 +311,6 @@
         remote(gxw.at[there(ah, bh)], orecv.at[here(ah, bh)], ret_ss.at[ah * 2 + bh], ret_rs.at[ah * 2 + bh], from_window(ah, bh))
         for ah, bh in quarters
     ]
-    for c in ret_copies:
-        c.start()
 
     for c in halo + [core_rs_copy]:
         c.wait_send()
@@ -329,17 +336,21 @@
     for c in ta_out:
         c.start()
 
-    @pl.loop(1, NXY)
-    def _(o):
-        xy_copy(o).wait_recv()
-
-    acc = xy_f[p]
-    for o in range(NXY - 1):
-        acc += xy_r[o].astype(F32)
-    za[zr] = acc.astype(BF)
     za_out, za_in = spread(za, zr, za_ss, za_rs, zr_peer, 4)
-    for c in za_out:
-        c.start()
+
+    @pl.when(owner)
+    def _():
+        for j in range(NXY):
+            @pl.when(p != j)
+            def _(j=j):
+                remote(xy_s.at[0], xy_r.at[j], xy_ss.at[0], xy_rs.at[j], core_peer).wait_recv()
+
+        acc = xy_f[w]
+        for j in range(NXY):
+            acc += xy_r[j].astype(F32)
+        za[zr] = acc.astype(BF)
+        for c in za_out:
+            c.start()
 
     for c in ta_in:
         c.wait_recv()
@@ -350,26 +361,24 @@
     tb_out, tb_in = spread(tb, zhalf, tb_ss, tb_rs, lambda o: far_half, 2)
     tb_out[0].start()
 
-    for c in za_in:
-        c.wait_recv()
-    acc = za[0].astype(F32)
-    for j in range(1, 4):
-        acc += za[j].astype(F32)
-    zb[zq] = acc.astype(BF)
     zb_out, zb_in = spread(zb, zq, zb_ss, zb_rs, zq_peer, 4)
-    for c in zb_out:
+
+    @pl.when(owner)
+    def _():
+        for c in za_in:
+            c.wait_recv()
+        acc = za[0].astype(F32)
+        for j in range(1, 4):
+            acc += za[j].astype(F32)
+        zb[zq] = acc.astype(BF)
+        for c in zb_out:
+            c.start()
+
+    for c in ret_copies:
         c.start()
 
     tb_in[0].wait_recv()
-    tpiece = tb[0].astype(F32) + tb[1].astype(F32)
-    tpiece_low = tpiece.astype(BF)
-    tpiece = tpiece_low.astype(F32)
-    squares = jnp.sum(jnp.sum(tpiece * tpiece, axis=1, keepdims=True), axis=0, keepdims=True)
-    sq[mine] = jnp.broadcast_to(squares, (1, 128))
-    sq_out, sq_in = spread(sq, mine, sq_ss, sq_rs, sq_peer, 4)
-    for c in sq_out:
-        c.start()
-    tfin[cx] = tpiece_low
+    tfin[cx] = (tb[0].astype(F32) + tb[1].astype(F32)).astype(BF)
 
     def tcag_copy(o):
         _, device = cx_peer(o)
@@ -379,79 +388,90 @@
     def _(o):
         tcag_copy(o).start()
 
+    for n in range(PIECES):
+        at, c = xy_copy(n)
+
+        @pl.when(p != at)
+        def _(c=c):
+            c.wait_send()
+
+    @pl.loop(1, NCX)
+    def _(o):
+        tcx_copy(o).wait_send()
+
+    for c in ta_out + tb_out:
+        c.wait_send()
+
+    @pl.loop(1, NCX)
+    def _(o):
+        other = lax.rem(cx + NCX - o, NCX)
+        slot = tfin.at[other]
+        remote(slot, slot, tcag_ss.at[o - 1], tcag_rs.at[o - 1], cx_peer(o)[1]).wait_recv()
+
+    def squares_of(value):
+        return jnp.sum(jnp.sum(value * value, axis=1, keepdims=True), axis=0, keepdims=True)
+
+    band = mtm(trows_ref[...], tfin[...].reshape(128, 384))
+    sq[lat] = jnp.broadcast_to(squares_of(band), (1, 128))
+    sq_out, sq_in = spread(sq, lat, sq_ss, sq_rs, lat_peer, NLAT)
+    for c in sq_out:
+        c.start()
+
+    def xyag_copy(o):
+        _, device = xy_peer(o)
+        return remote(fin.at[core, w], fin.at[core, w], xyag_ss.at[o - 1], xyag_rs.at[w], device)
+
+    @pl.when(owner)
+    def _():
+        for c in za_out:
+            c.wait_send()
+        for c in zb_in:
+            c.wait_recv()
+        acc = zb[0].astype(F32)
+        for j in range(1, 4):
+            acc += zb[j].astype(F32)
+        fin[core, w] = acc.astype(BF)
+
+        @pl.loop(1, NXY)
+        def _(o):
+            xyag_copy(o).start()
+
     for c in ret_copies:
         c.wait()
     out_x[...] = (own_g[...].astype(F32) + orecv[...].astype(F32)).astype(BF)
 
-    @pl.loop(1, NXY)
-    def _(o):
-        xy_copy(o).wait_send()
-
     @pl.loop(1, NCX)
     def _(o):
-        tcx_copy(o).wait_send()
-
-    for c in ta_out + za_out + tb_out:
-        c.wait_send()
-
-    for c in zb_in:
-        c.wait_recv()
-    acc = zb[0].astype(F32)
-    for j in range(1, 4):
-        acc += zb[j].astype(F32)
-    piece[...] = acc
+        tcag_copy(o).wait_send()
+
+    @pl.when(owner)
+    def _():
+        for c in zb_out:
+            c.wait_send()
+
+    for n in range(PIECES):
+        at, device = place(n)
+
+        @pl.when(p != at)
+        def _(n=n, device=device):
+            slot = fin.at[core, n]
+            remote(slot, slot, xyag_ss.at[0], xyag_rs.at[n], device).wait_recv()
+
+    cag = remote(fin.at[core], fin.at[core], cag_ss, cag_rs, core_peer)
+    cag.start()
+
+    @pl.when(owner)
+    def _():
+        @pl.loop(1, NXY)
+        def _(o):
+            xyag_copy(o).wait_send()
+
     for c in sq_in:
         c.wait_recv()
-    both = (sq[0] + sq[1]) + (sq[2] + sq[3])
-    both_hi = both.astype(BF).astype(F32)
-    both_mid = (both - both_hi).astype(BF).astype(F32)
-    both_lo = both - both_hi - both_mid
-    lane = lax.broadcasted_iota(jnp.int32, (1, 128), 1)
-    piece[13:14, 0:128] = jnp.where(
-        lane == 0, both_hi, jnp.where(lane == 1, both_mid, jnp.where(lane == 2, both_lo, 0.0))
-    )
-    fin[core, p] = piece[...].astype(BF)
-
-    def xyag_copy(o):
-        _, device = xy_peer(o)
-        return remote(fin.at[core, p], fin.at[core, p], xyag_ss.at[o - 1], xyag_rs.at[o - 1], device)
-
-    @pl.loop(1, NXY)
-    def _(o):
-        xyag_copy(o).start()
-
-    @pl.loop(1, NCX)
-    def _(o):
-        other = lax.rem(cx + NCX - o, NCX)
-        slot = tfin.at[other]
-        remote(slot, slot, tcag_ss.at[o - 1], tcag_rs.at[o - 1], cx_peer(o)[1]).wait_recv()
-
-    band = mtm(trows_ref[...], tfin[...].reshape(128, 384))
-
-    @pl.loop(1, NCX)
-    def _(o):
-        tcag_copy(o).wait_send()
-
-    for c in zb_out + sq_out:
-        c.wait_send()
-
-    @pl.loop(1, NXY)
-    def _(o):
-        other = lax.rem(p + NXY - o, NXY)
-        slot = fin.at[core, other]
-        remote(slot, slot, xyag_ss.at[o - 1], xyag_rs.at[o - 1], xy_peer(o)[1]).wait_recv()
-
-    cag = remote(fin.at[core], fin.at[core], cag_ss, cag_rs, core_peer)
-    cag.start()
-
-    @pl.loop(1, NXY)
-    def _(o):
-        xyag_copy(o).wait_send()
-
-    shares = jnp.zeros((1, 128), F32)
-    for j in range(NXY):
-        shares += fin[core, j, 13:14, 0:128].astype(F32)
-    total = jnp.sum(shares, axis=1, keepdims=True)
+    total = sq[0]
+    for j in range(1, NLAT):
+        total += sq[j]
+    total = total[:, 0:1]
     band = band * (1.0 / jnp.sqrt(total / (NLAT * 6 * 3312) + EPS_RMS))
     for l_s in range(2):
         for a_s in range(6):
@@ -461,13 +481,12 @@
                 t1[:, pl.ds(off, 138)] = band[la * 6:la * 6 + 6, l_t * 138:l_t * 138 + 138]
     for h in range(6):
         out_table[h] = t1[h:h + 1, :]
-
-    def squares_of(value):
-        return jnp.sum(jnp.sum(value * value, axis=1, keepdims=True), axis=0, keepdims=True)
+    for c in sq_out:
+        c.wait_send()
 
     def part(which_core):
-        value = mm(rows_ref[...], fin[which_core].reshape(256, 384))
-        return value, squares_of(value[:, 0:192]), squares_of(value[:, 192:384]), fin[which_core, 0, 12:13, 0:192].astype(F32)
+        value = fin[which_core, 0:PIECES - 1].reshape(192, 384).astype(F32)
+        return value, squares_of(value[:, 0:192]), squares_of(value[:, 192:384]), fin[which_core, PIECES - 1, 0:1, 0:192].astype(F32)
 
     own = part(core)
     other_half = fin.at[1 - core]
@@ -510,20 +529,20 @@
     ]
     scratch = [pltpu.VMEM(o.shape, o.dtype) for o in operands[2:]] + [
         pltpu.VMEM((6, 12, 2, 192), BF), pltpu.VMEM((6, 12, 2, 192), BF), pltpu.VMEM((1, 144), F32), pltpu.VMEM((1, 144), F32),
-        pltpu.VMEM((6, 12, 2, 192), BF), pltpu.VMEM((6, 12, 2, 192), BF), pltpu.VMEM((6, 12, 2, 192), BF), pltpu.VMEM((6, 12, 2, 192), BF),
-        pltpu.VMEM((144, 192), BF), pltpu.VMEM((144, 192), BF), pltpu.VMEM((144, 192), BF),
+        pltpu.VMEM((6, 12, 3, 2, 128), BF), pltpu.VMEM((6, 12, 3, 2, 128), BF),
+        pltpu.VMEM((6, 12, 2, 192), BF), pltpu.VMEM((6, 12, 2, 192), BF),
+        pltpu.VMEM((144, 384), BF), pltpu.VMEM((144, 192), BF),
         pltpu.VMEM((6, 3312), F32), pltpu.VMEM((72, 384), F32), pltpu.VMEM((864, 144), F32),
-        pltpu.VMEM((2, 256, 384), F32), pltpu.VMEM((256, 384), BF), pltpu.VMEM((256, 384), BF),
-        pltpu.VMEM((16, 16, 384), F32), pltpu.VMEM((16, 16, 384), BF), pltpu.VMEM((15, 16, 384), BF),
-        pltpu.VMEM((4, 16, 384), BF), pltpu.VMEM((4, 16, 384), BF), pltpu.VMEM((16, 384), F32),
-        pltpu.VMEM((2, 16, 16, 384), BF),
+        pltpu.VMEM((2, 192, 384), F32), pltpu.VMEM((192, 384), BF), pltpu.VMEM((192, 384), BF),
+        pltpu.VMEM((PIECES, 16, 384), F32), pltpu.VMEM((PIECES, 16, 384), BF), pltpu.VMEM((16, 16, 384), BF),
+        pltpu.VMEM((4, 16, 384), BF), pltpu.VMEM((4, 16, 384), BF), pltpu.VMEM((2, PIECES, 16, 384), BF),
         pltpu.VMEM((8, 16, 384), BF), pltpu.VMEM((7, 16, 384), BF),
         pltpu.VMEM((4, 16, 384), BF), pltpu.VMEM((2, 16, 384), BF),
-        pltpu.VMEM((8, 16, 384), BF), pltpu.VMEM((4, 1, 128), F32),
-        dma((14,)), dma, dma, dma((8,)), dma((8,)), dma((4,)), dma((4,)), dma, dma,
-        dma((15,)), dma((15,)), dma((3,)), dma((3,)), dma((3,)), dma((3,)),
-        dma((15,)), dma((15,)), dma, dma,
-        dma((7,)), dma((7,)), dma((3,)), dma((3,)), dma((1,)), dma((1,)), dma((7,)), dma((7,)), dma((3,)), dma((3,)),
+        pltpu.VMEM((8, 16, 384), BF), pltpu.VMEM((NLAT, 1, 128), F32),
+        dma((13,)), dma, dma, dma((4,)), dma((4,)), dma((4,)), dma((4,)), dma, dma,
+        dma((PIECES,)), dma((16,)), dma((3,)), dma((3,)), dma((3,)), dma((3,)),
+        dma((15,)), dma((PIECES,)), dma, dma,
+        dma((7,)), dma((7,)), dma((3,)), dma((3,)), dma((1,)), dma((1,)), dma((7,)), dma((7,)), dma((7,)), dma((7,)),
     ]
     shapes = (
         jax.ShapeDtypeStruct((6, 12, 2, 192), BF),

time: 64.1 us -> 60.8 us (0.949)
  Pallas kernels: 63.4 us -> 60 us
    pallas_call x1, Pallas kernels: 62.4 us -> 59.1 us  [on_device(): pl.pallas_call(kernel, out_shape=shapes, in_specs=[hbm] * len(operands),...]
where the time goes in v4:
time: 60.8 us; the launch traced here: 60.7 us
  Pallas kernels  60 us (99%)
  between operations  0.64 us (1%)
    pallas_call x1, Pallas kernels, on_device(): pl.pallas_call(kernel, out_shape=shapes, in_specs=[hbm] * len(operands),...  59.1 us

profile of v4, /device:TPU:1, one launch (start us, length us, event | category | flops | bytes accessed | tf_op | source)
XLA Modules:
  0.0 60.7 jit_solution(16910382168159588479)
XLA Ops:
  0.6 59.1 %swin_backward.1 = (bf16[6,12,2,192]{3,2,1,0:T(2,128)(2,1)S(1)}, f32[192,576]{1,0:T(8,128)S(1)}, f32[192,192]{1,0:T(8,128)S(1)}, f32[1,192]{1,0:T(1,128)S(1)}, f32[6,1,3312]{2,1,0:T(1,128)S(1)}) custom-call(bf16[6,12,2,192]{3,2,1,0:T(2,128)(2,1)} %bitcast.9, bf16[6,12,2,192]{3,2,1,0:T(2,128)(2,1)} %bitcast.10, f32[1,192]{1,0:T(1,128)} %bitcast.12, ...), custom_call_target="tpu_custom_call" | custom-call | tf_op jit(solution)/shard_map/swin_backward/pallas_call | solution.py:554
  59.7 0.9 %hand_over.1 = (bf16[6,12,2,192]{3,2,1,0:T(2,128)(2,1)}, f32[192,576]{1,0:T(8,128)}, f32[192,192]{1,0:T(8,128)}, f32[1,192]{1,0:T(1,128)}, f32[6,1,3312]{2,1,0:T(1,128)}) custom-call(bf16[6,12,2,192]{3,2,1,0:T(2,128)(2,1)S(1)} %get-tuple-element.15.refs_0_, f32[192,576]{1,0:T(8,128)S(1)} %get-tuple-element.16.refs_1_, ...), custom_call_target="tpu_custom_call" | custom-call | tf_op jit(solution)/shard_map/hand_over/pallas_call | solution.py:565

commit v5 on v4

--- a/solution.py
+++ b/solution.py
@@ -70,7 +70,7 @@
     tcx_s, tcx_r, ta, tb, tfin, sq,
     load_sem, reg_ss, reg_rs, halo_ss, halo_rs, ret_ss, ret_rs, core_ss, core_rs, xy_ss, xy_rs, za_ss, za_rs, zb_ss, zb_rs,
     xyag_ss, xyag_rs, cag_ss, cag_rs,
-    tcx_ss, tcx_rs, ta_ss, ta_rs, tb_ss, tb_rs, tcag_ss, tcag_rs, sq_ss, sq_rs,
+    tcx_ss, tcx_rs, ta_ss, ta_rs, tb_ss, tb_rs, tcag_ss, tcag_rs, sq_ss, sq_rs, far_sem, band_sem,
 ):
     lat = lax.axis_index("lat")
     lon = lax.axis_index("lon")
@@ -131,22 +131,6 @@
     def greet(device):
         pl.semaphore_signal(barrier, inc=1, device_id=device, device_id_type=MESH)
 
-    quarters = ((1, 1), (1, 0), (0, 1), (0, 0))
-    for ah, bh in quarters:
-        greet(from_window(ah, bh))
-        greet(to_window(ah, bh))
-    greet(core_peer)
-
-    @pl.loop(1, NXY)
-    def _(o):
-        greet(xy_peer(o)[1])
-
-    for o in range(1, 4):
-        greet(zr_peer(o))
-        greet(zq_peer(o))
-        greet((lat, lon_of(lax.rem(x + o, NX), z_lo, 1 - core)))
-        greet((lax.rem(y + o, NY) * ZHI + 1 - z_hi, lon))
-
     pairs = (
         (x_hbm, own_x), (g_hbm, own_g), (regions_hbm, regions_ref), (col_hbm, col_ref), (lev_hbm, lev_ref),
         (table_hbm, table_ref), (shift_hbm, shift_ref), (rep_hbm, rep_ref), (heads_hbm, heads_ref),
@@ -154,7 +138,25 @@
         (trows_hbm, trows_ref),
     )
     loads = [pltpu.make_async_copy(src, dst, load_sem.at[n]) for n, (src, dst) in enumerate(pairs)]
-    for c in loads:
+    for c in loads[:2]:
+        c.start()
+
+    quarters = ((1, 1), (1, 0), (0, 1), (0, 0))
+    for ah, bh in quarters:
+        greet(from_window(ah, bh))
+    for ah, bh in quarters:
+        greet(to_window(ah, bh))
+    greet(zq_peer(1))
+    greet(zq_peer(3))
+    steps = [(i, j) for i in range(NX) for j in range(NY) if (i, j) != (0, 0)]
+    for i, j in sorted(steps, key=lambda d: -(min(d[0], NX - d[0]) + min(d[1], NY - d[1]))):
+        greet((lax.rem(y + j, NY) * ZHI + z_hi, lon_of(lax.rem(x + i, NX), z_lo, core)))
+    for o in range(1, 4):
+        greet((lat, lon_of(lax.rem(x + o, NX), z_lo, 1 - core)))
+    for o in range(1, 4):
+        greet(zr_peer(o))
+    greet(core_peer)
+    for c in loads[2:]:
         c.start()
 
     for c in loads[:5]:
@@ -169,7 +171,7 @@
     pack[:, :, 1] = own_g[:, :, :, 0:128]
     pack[:, :, 2] = jnp.concatenate([own_x[:, :, :, 128:192], own_g[:, :, :, 128:192]], axis=-1)
 
-    pl.semaphore_wait(barrier, 8 + 1 + (NXY - 1) + 12)
+    pl.semaphore_wait(barrier, 8 + 2 + (NXY - 1) + 3 + 3 + 1)
 
     def remote(src, dst, ss, rs, device):
         return pltpu.make_async_remote_copy(
@@ -190,6 +192,7 @@
         ))
     for c in halo:
         c.start()
+    pl.semaphore_signal(far_sem, inc=1, device_id=zq_peer(3), device_id_type=MESH)
 
     for c in loads[5:]:
         c.wait()
@@ -266,19 +269,6 @@
 
     grad_normed = mmt(gpi, wqkv_ref[...])
     gain_raw = jnp.sum(grad_normed * standard, axis=0, keepdims=True)
-    t_acc = jnp.zeros((72, 384), F32)
-    for b in range(12):
-        t_acc += mm(gs_low[b * 72:(b + 1) * 72, :], shift_ref[b])
-    tcx_s[...] = mm(trows_ref[...], t_acc.astype(BF)).astype(BF).reshape(8, 16, 384)
-
-    def tcx_copy(o):
-        other, device = cx_peer(o)
-        return remote(tcx_s.at[other], tcx_r.at[o - 1], tcx_ss.at[o - 1], tcx_rs.at[o - 1], device)
-
-    @pl.loop(1, NCX)
-    def _(o):
-        tcx_copy(o).start()
-
     core_rs_copy.wait_recv()
     both_cores = main_f[core] + main_r[...].astype(F32)
     xy_f[0:PIECES - 1] = both_cores.reshape(PIECES - 1, 16, 384)
@@ -297,6 +287,19 @@
         @pl.when(p != at)
         def _(c=c):
             c.start()
+
+    t_acc = jnp.zeros((72, 384), F32)
+    for b in range(12):
+        t_acc += mm(gs_low[b * 72:(b + 1) * 72, :], shift_ref[b])
+    tcx_s[...] = mm(trows_ref[...], t_acc.astype(BF)).astype(BF).reshape(8, 16, 384)
+
+    def tcx_copy(o):
+        other, device = cx_peer(o)
+        return remote(tcx_s.at[other], tcx_r.at[o - 1], tcx_ss.at[o - 1], tcx_rs.at[o - 1], device)
+
+    @pl.loop(1, NCX)
+    def _(o):
+        tcx_copy(o).start()
 
     grad_std = grad_normed * gain
     grad_x = inv_std * (
@@ -361,6 +364,12 @@
     tb_out, tb_in = spread(tb, zhalf, tb_ss, tb_rs, lambda o: far_half, 2)
     tb_out[0].start()
 
+    pl.semaphore_wait(far_sem, 1)
+    for o in range(1, NY):
+        pl.semaphore_signal(
+            band_sem, inc=1, device_id=(lax.rem(y + o, NY) * ZHI + z_hi, lon), device_id_type=MESH
+        )
+
     zb_out, zb_in = spread(zb, zq, zb_ss, zb_rs, zq_peer, 4)
 
     @pl.when(owner)
@@ -371,7 +380,7 @@
         for j in range(1, 4):
             acc += za[j].astype(F32)
         zb[zq] = acc.astype(BF)
-        for c in zb_out:
+        for c in (zb_out[1], zb_out[0], zb_out[2]):
             c.start()
 
     for c in ret_copies:
@@ -414,6 +423,7 @@
     band = mtm(trows_ref[...], tfin[...].reshape(128, 384))
     sq[lat] = jnp.broadcast_to(squares_of(band), (1, 128))
     sq_out, sq_in = spread(sq, lat, sq_ss, sq_rs, lat_peer, NLAT)
+    pl.semaphore_wait(band_sem, NY - 1)
     for c in sq_out:
         c.start()
 
@@ -543,6 +553,7 @@
         dma((PIECES,)), dma((16,)), dma((3,)), dma((3,)), dma((3,)), dma((3,)),
         dma((15,)), dma((PIECES,)), dma, dma,
         dma((7,)), dma((7,)), dma((3,)), dma((3,)), dma((1,)), dma((1,)), dma((7,)), dma((7,)), dma((7,)), dma((7,)),
+        pltpu.SemaphoreType.REGULAR, pltpu.SemaphoreType.REGULAR,
     ]
     shapes = (
         jax.ShapeDtypeStruct((6, 12, 2, 192), BF),

time: 60.8 us -> 60 us (0.987)
  Pallas kernels: 60 us -> 59.2 us
    pallas_call x1, Pallas kernels: 59.1 us -> 58.3 us  [on_device(): pl.pallas_call(kernel, out_shape=shapes, in_specs=[hbm] * len(operands),...]
where the time goes in v5:
time: 60 us; the launch traced here: 59.8 us
  Pallas kernels  59.2 us (99%)
  between operations  0.64 us (1%)
    pallas_call x1, Pallas kernels, on_device(): pl.pallas_call(kernel, out_shape=shapes, in_specs=[hbm] * len(operands),...  58.3 us

profile of v5, /device:TPU:1, one launch (start us, length us, event | category | flops | bytes accessed | tf_op | source)
XLA Modules:
  0.0 59.8 jit_solution(3448795503365264470)
XLA Ops:
  0.6 58.3 %swin_backward.1 = (bf16[6,12,2,192]{3,2,1,0:T(2,128)(2,1)S(1)}, f32[192,576]{1,0:T(8,128)S(1)}, f32[192,192]{1,0:T(8,128)S(1)}, f32[1,192]{1,0:T(1,128)S(1)}, f32[6,1,3312]{2,1,0:T(1,128)S(1)}) custom-call(bf16[6,12,2,192]{3,2,1,0:T(2,128)(2,1)} %bitcast.9, bf16[6,12,2,192]{3,2,1,0:T(2,128)(2,1)} %bitcast.10, f32[1,192]{1,0:T(1,128)} %bitcast.12, ...), custom_call_target="tpu_custom_call" | custom-call | tf_op jit(solution)/shard_map/swin_backward/pallas_call | solution.py:565
  58.9 0.9 %hand_over.1 = (bf16[6,12,2,192]{3,2,1,0:T(2,128)(2,1)}, f32[192,576]{1,0:T(8,128)}, f32[192,192]{1,0:T(8,128)}, f32[1,192]{1,0:T(1,128)}, f32[6,1,3312]{2,1,0:T(1,128)}) custom-call(bf16[6,12,2,192]{3,2,1,0:T(2,128)(2,1)S(1)} %get-tuple-element.15.refs_0_, f32[192,576]{1,0:T(8,128)S(1)} %get-tuple-element.16.refs_1_, ...), custom_call_target="tpu_custom_call" | custom-call | tf_op jit(solution)/shard_map/hand_over/pallas_call | solution.py:576
